TPU v7x, 32 devices: a whole 2x2x4 slice. The times are simulated.
32 devices in a mesh: ctx: 8 (over y, x, core), exp: 4 (over z).
Axes of the slice: x: 2, y: 2, z: 4, core: 2. Of those that a mesh axis runs over, the one named last changes fastest.
Arguments:
- tokens: bfloat16 [4, 1024, 1536], P('exp', 'ctx'), may hold values from -6 to 6
- out_grad: bfloat16 [4, 1024, 1536], P('exp', 'ctx'), may hold values from -6 to 6
- attn_gain: float32 [1536], replicated, may hold values from 0.5 to 1.5
- moe_gain: float32 [1536], replicated, may hold values from 0.5 to 1.5
- w_query: bfloat16 [1536, 1536], P(('ctx', 'exp')), may hold values from -0.15625 to 0.15625
- lock_projection: bfloat16 [1536, 512], P(('ctx', 'exp')), may hold values from -0.15625 to 0.15625
- content_projection: bfloat16 [1536, 512], P(('ctx', 'exp')), may hold values from -0.15625 to 0.15625
- w_out: bfloat16 [1536, 1536], P(('ctx', 'exp')), may hold values from -0.875 to 0.875
- sigmoid_matrices: bfloat16 [40, 1536, 512], P('exp'), may hold values from -0.15625 to 0.15625
- widener_matrices: bfloat16 [40, 1536, 512], P('exp'), may hold values from -0.15625 to 0.15625
- reducer_matrices: bfloat16 [40, 512, 1536], P('exp'), may hold values from -0.5 to 0.5
- segment_ids: int32 [4, 1024], P('exp', 'ctx'), may hold values from 0 to 2, as said below
- expert_routes: int32 [4, 1024, 8], P('exp', 'ctx'), may hold values from 0 to 39, all different within a row; in each aligned block of 128 rows (0 to 127, 128 to 255, ..., all dimensions but the last counted through in order) at most 48 rows name the same one
- route_weights: float32 [4, 1024, 8], P('exp', 'ctx'), may hold values from 0.06 to 0.2
- adapter_index: int32 [4], replicated, may hold values from 0 to 7
- query_first: bfloat16 [8, 16, 1536], replicated, may hold values from -0.15625 to 0.15625
- query_second: bfloat16 [8, 16, 1536], replicated, may hold values from -0.75 to 0.75
- key_first: bfloat16 [8, 16, 1536], replicated, may hold values from -0.15625 to 0.15625
- lock_final_matrices: bfloat16 [8, 16, 512], replicated, may hold values from -0.75 to 0.75
- value_first: bfloat16 [8, 16, 1536], replicated, may hold values from -0.15625 to 0.15625
- content_final_matrices: bfloat16 [8, 16, 512], replicated, may hold values from -0.75 to 0.75
- output_first: bfloat16 [8, 16, 1536], replicated, may hold values from -0.15625 to 0.15625
- output_second: bfloat16 [8, 16, 1536], replicated, may hold values from -1.5 to 1.5
- gate_first: bfloat16 [8, 40, 16, 1536], P(None, 'exp'), may hold values from -0.15625 to 0.15625
- gate_second: bfloat16 [8, 40, 16, 512], P(None, 'exp'), may hold values from -0.75 to 0.75
- upward_first: bfloat16 [8, 40, 16, 1536], P(None, 'exp'), may hold values from -0.15625 to 0.15625
- upward_second: bfloat16 [8, 40, 16, 512], P(None, 'exp'), may hold values from -0.75 to 0.75
- down_first: bfloat16 [8, 40, 16, 512], P(None, 'exp'), may hold values from -0.25 to 0.25
- down_second: bfloat16 [8, 40, 16, 1536], P(None, 'exp'), may hold values from -1.5 to 1.5
Outputs:
- block_out: bfloat16 [4, 1024, 1536], P('exp', 'ctx')
- tokens_grad: bfloat16 [4, 1024, 1536], P('exp', 'ctx')
- grad_query_first: float32 [8, 16, 1536], replicated
- grad_query_second: float32 [8, 16, 1536], replicated
- grad_key_first: float32 [8, 16, 1536], replicated
- grad_key_second: float32 [8, 16, 512], replicated
- grad_value_first: float32 [8, 16, 1536], replicated
- grad_value_second: float32 [8, 16, 512], replicated
- grad_output_first: float32 [8, 16, 1536], replicated
- grad_output_second: float32 [8, 16, 1536], replicated
- grad_gate_first: float32 [8, 40, 16, 1536], P(None, 'exp', None, 'ctx')
- grad_gate_second: float32 [8, 40, 16, 512], P(None, 'exp', None, 'ctx')
- grad_upward_first: float32 [8, 40, 16, 1536], P(None, 'exp', None, 'ctx')
- grad_upward_second: float32 [8, 40, 16, 512], P(None, 'exp', None, 'ctx')
- grad_down_first: float32 [8, 40, 16, 512], P(None, 'exp', None, 'ctx')
- grad_down_second: float32 [8, 40, 16, 1536], P(None, 'exp', None, 'ctx')
Inputs may be any that keep to these rules, and one draw needn't show every extreme that they name: `segment_ids`: in each group the prompt (segment 0) is the first 512 to 576 tokens; then continuations 1 to 2 follow in order, none empty. `expert_routes`: A token names 8 different experts. Among the 128 tokens of one group on one index of ctx (aligned blocks), no expert is named more than 48 times, and in some blocks one is named exactly 48 times.
All inputs are finite; a program needn't handle non-finite values.
Results may differ from a plain program's by a relative error of at most 0.024.
Values may be sent and summed in bfloat16 or wider, within the bound.
No kernel may reach another device: no remote copies, remote signals or barrier semaphores. Data moves between devices by JAX's collectives and lax.ppermute only.
A program may use at most 384 MiB of HBM per device.

v0:
```python
import jax
import jax.numpy as jnp
from jax import lax
from jax.sharding import PartitionSpec as P

ASKING_ATTENDERS = 24
PAIRED_ATTENDERS = 8
ATTENTION_EXTENT = 64
EXPERTS = 40
TOPK = 8
NUM_CHOICES_X = 8
CAP = 48


EPS = 1e-06
LOW_FACTORED = 2.0
MASKED_FLOOR = -1e30
SCALE = 0.125
STRICT_ACCURACY = lax.Precision.HIGHEST


def matrix_produce(left, right):
    return jnp.dot(left, right, preferred_element_type=jnp.float32)


def matrix_prefix(left, right):
    return lax.dot_general(
        left, right, (((0,), (0,)), ((), ())), preferred_element_type=jnp.float32
    )


def matrix_suffix(left, right):
    return lax.dot_general(
        left, right, (((1,), (1,)), ((), ())), preferred_element_type=jnp.float32
    )


def normed(content_entries, gain):
    factor = lax.rsqrt(jnp.mean(content_entries * content_entries, axis=-1, keepdims=True) + EPS)
    return (content_entries * factor * gain, factor)


def norm_back(content_entries, factor, gain, adjoint_signal):
    weighted = adjoint_signal * gain
    central_values = jnp.mean(weighted * content_entries, axis=-1, keepdims=True)
    return factor * (weighted - content_entries * factor * factor * central_values)


def adapted(record_lines, frozen_plain, first, closing_factor):
    central_values = matrix_suffix(record_lines, first).astype(jnp.bfloat16)
    return (
        matrix_produce(record_lines, frozen_plain)
        + LOW_FACTORED * matrix_produce(central_values, closing_factor),
        central_values,
    )


def adapted_back(adjoint_signal, record_lines, central_values, frozen_plain, first, closing_factor):
    adjoint_final_factor = LOW_FACTORED * matrix_prefix(central_values, adjoint_signal)
    adjoint_central = (LOW_FACTORED * matrix_suffix(adjoint_signal, closing_factor)).astype(
        jnp.bfloat16
    )
    grad_first = matrix_prefix(adjoint_central, record_lines)
    grad_rows = matrix_suffix(adjoint_signal, frozen_plain) + matrix_produce(adjoint_central, first)
    return (grad_rows, grad_first, adjoint_final_factor)


def permitted(query_place, query_segment, key_place, key_segment):
    later = key_place[None, :] <= query_place[:, None]
    same = (key_segment[None, :] == query_segment[:, None]) | (key_segment[None, :] == 0.0)
    return later & same


def head_major(rows, heads):
    return jnp.transpose(rows.reshape(rows.shape[0], heads, -1), (1, 0, 2))


def scores_of(question_heads, lock_heads):
    return (
        jnp.einsum("hgtd,hkd->hgtk", question_heads, lock_heads, preferred_element_type=jnp.float32)
        * SCALE
    )


def attend_block(carry, lock_heads, content_heads, key_segment, start, context):
    question_heads, query_place, query_segment = context

    def attend_compute(state):
        running, total, accumulated = state
        count = lock_heads.shape[1]
        key_place = start + jnp.arange(count, dtype=jnp.int32)
        allowed = permitted(query_place, query_segment, key_place, key_segment.astype(jnp.float32))
        masked = jnp.where(allowed, scores_of(question_heads, lock_heads), MASKED_FLOOR)
        newest = jnp.maximum(running, jnp.max(masked, axis=-1))
        weights = jnp.where(allowed, jnp.exp(masked - newest[..., None]), 0.0)
        factor = jnp.exp(running - newest)
        total = total * factor + jnp.sum(weights, axis=-1)
        update = jnp.einsum(
            "hgtk,hkd->hgtd",
            weights.astype(jnp.bfloat16),
            content_heads,
            preferred_element_type=jnp.float32,
        )
        accumulated = accumulated * factor[..., None] + update
        return (newest, total, accumulated)

    def attend_unchanged(state):
        return state

    return lax.cond(start > query_place[-1], attend_unchanged, attend_compute, carry)


def attend_piece(carry, piece, start, block, context):
    key_rows, value_rows, key_segment = piece
    heads = context[0].shape[0]
    lock_heads = head_major(key_rows, heads)
    content_heads = head_major(value_rows, heads)
    count = key_rows.shape[0]
    number = count // block

    def block_step(state, index):
        offset = index * block
        return (
            attend_block(
                state,
                lax.dynamic_slice_in_dim(lock_heads, offset, block, 1),
                lax.dynamic_slice_in_dim(content_heads, offset, block, 1),
                lax.dynamic_slice_in_dim(key_segment, offset, block, 0),
                start + offset,
                context,
            ),
            None,
        )

    carry, unused = lax.scan(block_step, carry, jnp.arange(number, dtype=jnp.int32))
    return carry


def grads_block(grad_query, start, lock_heads, content_heads, key_segment, context):
    question_heads, query_place, query_segment, log_total, adjoint_heads, delta = context
    heads = lock_heads.shape[0]
    count = lock_heads.shape[1]
    extent = lock_heads.shape[2]

    def grads_compute(running_grad):
        key_place = start + jnp.arange(count, dtype=jnp.int32)
        allowed = permitted(query_place, query_segment, key_place, key_segment.astype(jnp.float32))
        weights = jnp.where(
            allowed, jnp.exp(scores_of(question_heads, lock_heads) - log_total[..., None]), 0.0
        )
        grad_weights = jnp.einsum(
            "hgtd,hkd->hgtk", adjoint_heads, content_heads, preferred_element_type=jnp.float32
        )
        grad_score = (weights * (grad_weights - delta[..., None])).astype(jnp.bfloat16)
        new_grad = running_grad + SCALE * jnp.einsum(
            "hgtk,hkd->hgtd", grad_score, lock_heads, preferred_element_type=jnp.float32
        )
        grad_keys = SCALE * jnp.einsum(
            "hgtk,hgtd->hkd", grad_score, question_heads, preferred_element_type=jnp.float32
        )
        grad_values = jnp.einsum(
            "hgtk,hgtd->hkd",
            weights.astype(jnp.bfloat16),
            adjoint_heads,
            preferred_element_type=jnp.float32,
        )
        return (new_grad, (grad_keys, grad_values))

    def grads_unchanged(running_grad):
        empty = jnp.zeros((heads, count, extent), jnp.float32)
        return (running_grad, (empty, empty))

    return lax.cond(start > query_place[-1], grads_unchanged, grads_compute, grad_query)


def body(
    tokens,
    out_grad,
    attn_gain,
    moe_gain,
    w_query,
    lock_projection,
    content_projection,
    w_out,
    sigmoid_matrices,
    widener_matrices,
    reducer_matrices,
    segment_ids,
    expert_routes,
    route_weights,
    adapter_index,
    query_first,
    query_second,
    key_first,
    lock_final_matrices,
    value_first,
    content_final_matrices,
    output_first,
    output_second,
    gate_first,
    gate_second,
    upward_first,
    upward_second,
    down_first,
    down_second,
):
    unique_one = jnp.float32
    rows_in = tokens[0].astype(unique_one)
    nearby_lines_set = rows_in.shape[0]
    width = rows_in.shape[1]
    exp_size = lax.axis_size("exp")
    local_experts = sigmoid_matrices.shape[0]
    attender_wise = ASKING_ATTENDERS // PAIRED_ATTENDERS
    adapter = adapter_index[lax.axis_index("exp")]

    def elected_ones(table):
        return lax.dynamic_index_in_dim(table, adapter, 0, keepdims=False)

    full_query, full_key, full_value, full_out = (
        lax.all_gather(w_query, ("ctx", "exp"), axis=0, tiled=True),
        lax.all_gather(lock_projection, ("ctx", "exp"), axis=0, tiled=True),
        lax.all_gather(content_projection, ("ctx", "exp"), axis=0, tiled=True),
        lax.all_gather(w_out, ("ctx", "exp"), axis=0, tiled=True),
    )
    normed_in_f, factor_in = normed(rows_in, attn_gain)
    normed_in = normed_in_f.astype(jnp.bfloat16)
    query_f, inner_query = adapted(
        normed_in, full_query, elected_ones(query_first), elected_ones(query_second)
    )
    key_f, inner_key = adapted(
        normed_in, full_key, elected_ones(key_first), elected_ones(lock_final_matrices)
    )
    value_f, inner_value = adapted(
        normed_in, full_value, elected_ones(value_first), elected_ones(content_final_matrices)
    )
    question_entries = query_f.astype(jnp.bfloat16)
    lock_entries = key_f.astype(jnp.bfloat16)
    content_entries = value_f.astype(jnp.bfloat16)
    question_heads = jnp.transpose(
        question_entries.reshape(
            nearby_lines_set, PAIRED_ATTENDERS, attender_wise, ATTENTION_EXTENT
        ),
        (1, 2, 0, 3),
    )
    query_place = lax.axis_index("ctx") * nearby_lines_set + jnp.arange(
        nearby_lines_set, dtype=jnp.int32
    )
    query_segment = segment_ids[0].astype(unique_one)
    segment_wire = segment_ids[0].astype(jnp.bfloat16)
    block = 2 * nearby_lines_set
    context = (question_heads, query_place, query_segment)
    start_state = (
        jnp.full((PAIRED_ATTENDERS, attender_wise, nearby_lines_set), MASKED_FLOOR, unique_one),
        jnp.zeros((PAIRED_ATTENDERS, attender_wise, nearby_lines_set), unique_one),
        jnp.zeros(
            (PAIRED_ATTENDERS, attender_wise, nearby_lines_set, ATTENTION_EXTENT), unique_one
        ),
    )
    key_source = (
        lax.all_gather(lock_entries, "ctx", axis=0, tiled=True),
        lax.all_gather(content_entries, "ctx", axis=0, tiled=True),
        lax.all_gather(segment_wire, "ctx", axis=0, tiled=True),
    )
    running, total, accumulated = attend_piece(start_state, key_source, 0, block, context)
    attended_heads = accumulated / total[..., None]
    log_total = running + jnp.log(total)
    attended = (
        jnp.transpose(attended_heads, (2, 0, 1, 3))
        .reshape(nearby_lines_set, ASKING_ATTENDERS * ATTENTION_EXTENT)
        .astype(jnp.bfloat16)
    )
    branch_f, inner_out = adapted(
        attended, full_out, elected_ones(output_first), elected_ones(output_second)
    )
    mid = rows_in + branch_f
    normed_mid_f, factor_mid = normed(mid, moe_gain)
    normed_mid = normed_mid_f.astype(jnp.bfloat16)
    flat_routes = expert_routes[0].reshape(-1)
    onehot = (flat_routes[:, None] == jnp.arange(EXPERTS, dtype=jnp.int32)[None, :]).astype(
        jnp.int32
    )
    slot_rank = jnp.sum((jnp.cumsum(onehot, axis=0) - 1) * onehot, axis=1)
    target = flat_routes * CAP + slot_rank

    def scatter_rows(record_lines):
        holding_place = jnp.zeros((EXPERTS * CAP, width), jnp.bfloat16).at[target].set(record_lines)
        return holding_place.reshape(exp_size, local_experts * CAP, width)

    received = lax.all_to_all(
        scatter_rows(jnp.repeat(normed_mid, TOPK, axis=0)),
        "exp",
        split_axis=0,
        concat_axis=0,
        tiled=True,
    ).reshape(exp_size, local_experts, CAP, width)
    chosen_gate_first = jnp.take(gate_first, adapter_index, axis=0)
    chosen_gate_second = jnp.take(gate_second, adapter_index, axis=0)
    chosen_upward_first = jnp.take(upward_first, adapter_index, axis=0)
    chosen_upward_second = jnp.take(upward_second, adapter_index, axis=0)
    chosen_down_first = jnp.take(down_first, adapter_index, axis=0)
    chosen_down_second = jnp.take(down_second, adapter_index, axis=0)
    central_sigmoid = jnp.einsum(
        "secd,serd->secr", received, chosen_gate_first, preferred_element_type=unique_one
    ).astype(jnp.bfloat16)
    sigmoidal_input = jnp.einsum(
        "secd,edf->secf", received, sigmoid_matrices, preferred_element_type=unique_one
    ) + LOW_FACTORED * jnp.einsum(
        "secr,serf->secf", central_sigmoid, chosen_gate_second, preferred_element_type=unique_one
    )
    central_widener = jnp.einsum(
        "secd,serd->secr", received, chosen_upward_first, preferred_element_type=unique_one
    ).astype(jnp.bfloat16)
    widening_input = jnp.einsum(
        "secd,edf->secf", received, widener_matrices, preferred_element_type=unique_one
    ) + LOW_FACTORED * jnp.einsum(
        "secr,serf->secf", central_widener, chosen_upward_second, preferred_element_type=unique_one
    )
    sigmoid_gate = jax.nn.sigmoid(sigmoidal_input)
    activated = sigmoidal_input * sigmoid_gate
    residual_flow = (activated * widening_input).astype(jnp.bfloat16)
    central_reducer = jnp.einsum(
        "secf,serf->secr", residual_flow, chosen_down_first, preferred_element_type=unique_one
    ).astype(jnp.bfloat16)
    specialist_answer = jnp.einsum(
        "secf,efd->secd", residual_flow, reducer_matrices, preferred_element_type=unique_one
    ) + LOW_FACTORED * jnp.einsum(
        "secr,serd->secd", central_reducer, chosen_down_second, preferred_element_type=unique_one
    )
    sent_back = lax.all_to_all(
        specialist_answer.astype(jnp.bfloat16).reshape(exp_size, local_experts * CAP, width),
        "exp",
        split_axis=0,
        concat_axis=0,
        tiled=True,
    )
    picked_rows = sent_back.reshape(EXPERTS * CAP, width)[target].reshape(
        nearby_lines_set, TOPK, width
    )
    gates = route_weights[0]
    mixture = jnp.sum(gates[..., None] * picked_rows, axis=1)
    block_out = (mid + mixture).astype(jnp.bfloat16)[None]
    grad_out = out_grad[0].astype(unique_one)
    grad_expert_rows = (
        (gates[..., None] * grad_out[:, None, :])
        .astype(jnp.bfloat16)
        .reshape(nearby_lines_set * TOPK, width)
    )
    grad_expert = lax.all_to_all(
        scatter_rows(grad_expert_rows), "exp", split_axis=0, concat_axis=0, tiled=True
    ).reshape(exp_size, local_experts, CAP, width)
    sender_reducer_final = LOW_FACTORED * jnp.einsum(
        "secr,secd->serd", central_reducer, grad_expert, preferred_element_type=unique_one
    )
    grad_inner_down = (
        LOW_FACTORED
        * jnp.einsum(
            "secd,serd->secr", grad_expert, chosen_down_second, preferred_element_type=unique_one
        )
    ).astype(jnp.bfloat16)
    source_down_first = jnp.einsum(
        "secr,secf->serf", grad_inner_down, residual_flow, preferred_element_type=unique_one
    )
    grad_hidden = jnp.einsum(
        "secd,efd->secf", grad_expert, reducer_matrices, preferred_element_type=unique_one
    ) + jnp.einsum(
        "secr,serf->secf", grad_inner_down, chosen_down_first, preferred_element_type=unique_one
    )
    grad_gate = (
        grad_hidden * widening_input * sigmoid_gate * (1.0 + sigmoidal_input * (1.0 - sigmoid_gate))
    ).astype(jnp.bfloat16)
    grad_upward = (grad_hidden * activated).astype(jnp.bfloat16)
    sender_sigmoid_final = LOW_FACTORED * jnp.einsum(
        "secr,secf->serf", central_sigmoid, grad_gate, preferred_element_type=unique_one
    )
    grad_inner_gate = (
        LOW_FACTORED
        * jnp.einsum(
            "secf,serf->secr", grad_gate, chosen_gate_second, preferred_element_type=unique_one
        )
    ).astype(jnp.bfloat16)
    source_gate_first = jnp.einsum(
        "secr,secd->serd", grad_inner_gate, received, preferred_element_type=unique_one
    )
    sender_widener_final = LOW_FACTORED * jnp.einsum(
        "secr,secf->serf", central_widener, grad_upward, preferred_element_type=unique_one
    )
    grad_inner_upward = (
        LOW_FACTORED
        * jnp.einsum(
            "secf,serf->secr", grad_upward, chosen_upward_second, preferred_element_type=unique_one
        )
    ).astype(jnp.bfloat16)
    source_upward_first = jnp.einsum(
        "secr,secd->serd", grad_inner_upward, received, preferred_element_type=unique_one
    )
    grad_received = jnp.einsum(
        "secf,edf->secd", grad_gate, sigmoid_matrices, preferred_element_type=unique_one
    ) + jnp.einsum(
        "secf,edf->secd", grad_upward, widener_matrices, preferred_element_type=unique_one
    )
    grad_received = (
        grad_received
        + jnp.einsum(
            "secr,serd->secd", grad_inner_gate, chosen_gate_first, preferred_element_type=unique_one
        )
        + jnp.einsum(
            "secr,serd->secd",
            grad_inner_upward,
            chosen_upward_first,
            preferred_element_type=unique_one,
        )
    )
    returned_grads = lax.all_to_all(
        grad_received.astype(jnp.bfloat16).reshape(exp_size, local_experts * CAP, width),
        "exp",
        split_axis=0,
        concat_axis=0,
        tiled=True,
    )
    grad_normed_mid = jnp.sum(
        returned_grads.reshape(EXPERTS * CAP, width)[target]
        .reshape(nearby_lines_set, TOPK, width)
        .astype(unique_one),
        axis=1,
    )
    source_onehot = (
        adapter_index[:, None] == jnp.arange(NUM_CHOICES_X, dtype=jnp.int32)[None, :]
    ).astype(unique_one)

    def to_table(source_grad):
        return jnp.einsum("sa,serx->aerx", source_onehot, source_grad, precision=STRICT_ACCURACY)

    expert_tables = (
        lax.psum_scatter(
            to_table(source_gate_first).astype(jnp.bfloat16), "ctx", scatter_dimension=3, tiled=True
        ).astype(jnp.float32),
        lax.psum_scatter(
            to_table(sender_sigmoid_final).astype(jnp.bfloat16),
            "ctx",
            scatter_dimension=3,
            tiled=True,
        ).astype(jnp.float32),
        lax.psum_scatter(
            to_table(source_upward_first).astype(jnp.bfloat16),
            "ctx",
            scatter_dimension=3,
            tiled=True,
        ).astype(jnp.float32),
        lax.psum_scatter(
            to_table(sender_widener_final).astype(jnp.bfloat16),
            "ctx",
            scatter_dimension=3,
            tiled=True,
        ).astype(jnp.float32),
        lax.psum_scatter(
            to_table(source_down_first).astype(jnp.bfloat16), "ctx", scatter_dimension=3, tiled=True
        ).astype(jnp.float32),
        lax.psum_scatter(
            to_table(sender_reducer_final).astype(jnp.bfloat16),
            "ctx",
            scatter_dimension=3,
            tiled=True,
        ).astype(jnp.float32),
    )
    grad_mid = grad_out + norm_back(mid, factor_mid, moe_gain, grad_normed_mid)
    grad_branch = grad_mid.astype(jnp.bfloat16)
    adjoint_mixed_wide, grad_output_first, grad_output_second = adapted_back(
        grad_branch,
        attended,
        inner_out,
        full_out,
        elected_ones(output_first),
        elected_ones(output_second),
    )
    adjoint_heads = jnp.transpose(
        adjoint_mixed_wide.astype(jnp.bfloat16).reshape(
            nearby_lines_set, PAIRED_ATTENDERS, attender_wise, ATTENTION_EXTENT
        ),
        (1, 2, 0, 3),
    )
    delta = jnp.sum(adjoint_heads * attended_heads, axis=-1)
    back_context = (question_heads, query_place, query_segment, log_total, adjoint_heads, delta)
    all_keys, all_values, all_segments = key_source
    all_key_heads = head_major(all_keys, PAIRED_ATTENDERS)
    all_value_heads = head_major(all_values, PAIRED_ATTENDERS)
    number = all_keys.shape[0] // block

    def adjoint_sweep(carry, index):
        offset = index * block
        return grads_block(
            carry,
            offset,
            lax.dynamic_slice_in_dim(all_key_heads, offset, block, 1),
            lax.dynamic_slice_in_dim(all_value_heads, offset, block, 1),
            lax.dynamic_slice_in_dim(all_segments, offset, block, 0),
            back_context,
        )

    grad_query_heads, lock_fragments = lax.scan(
        adjoint_sweep,
        jnp.zeros(
            (PAIRED_ATTENDERS, attender_wise, nearby_lines_set, ATTENTION_EXTENT), unique_one
        ),
        jnp.arange(number, dtype=jnp.int32),
    )
    key_rows_grad = jnp.transpose(lock_fragments[0], (0, 2, 1, 3)).reshape(
        -1, PAIRED_ATTENDERS * ATTENTION_EXTENT
    )
    value_rows_grad = jnp.transpose(lock_fragments[1], (0, 2, 1, 3)).reshape(
        -1, PAIRED_ATTENDERS * ATTENTION_EXTENT
    )
    grad_keys_f, grad_values_f = (
        lax.psum_scatter(
            key_rows_grad.astype(jnp.bfloat16), "ctx", scatter_dimension=0, tiled=True
        ).astype(jnp.float32),
        lax.psum_scatter(
            value_rows_grad.astype(jnp.bfloat16), "ctx", scatter_dimension=0, tiled=True
        ).astype(jnp.float32),
    )
    grad_queries = (
        jnp.transpose(grad_query_heads, (2, 0, 1, 3))
        .reshape(nearby_lines_set, ASKING_ATTENDERS * ATTENTION_EXTENT)
        .astype(jnp.bfloat16)
    )
    back_query, grad_query_first, grad_query_second = adapted_back(
        grad_queries,
        normed_in,
        inner_query,
        full_query,
        elected_ones(query_first),
        elected_ones(query_second),
    )
    back_key, grad_key_first, grad_key_second = adapted_back(
        grad_keys_f.astype(jnp.bfloat16),
        normed_in,
        inner_key,
        full_key,
        elected_ones(key_first),
        elected_ones(lock_final_matrices),
    )
    back_value, grad_value_first, grad_value_second = adapted_back(
        grad_values_f.astype(jnp.bfloat16),
        normed_in,
        inner_value,
        full_value,
        elected_ones(value_first),
        elected_ones(content_final_matrices),
    )
    grad_normed_in = back_query + back_key + back_value
    tokens_grad = (grad_mid + norm_back(rows_in, factor_in, attn_gain, grad_normed_in)).astype(
        jnp.bfloat16
    )[None]
    own_onehot = (jnp.arange(NUM_CHOICES_X, dtype=jnp.int32) == adapter).astype(unique_one)

    def placed_table(own_grad):
        return own_onehot[:, None, None] * own_grad[None]

    placed = [
        placed_table(own_grad)
        for own_grad in (
            grad_query_first,
            grad_query_second,
            grad_key_first,
            grad_key_second,
            grad_value_first,
            grad_value_second,
            grad_output_first,
            grad_output_second,
        )
    ]
    tables = lax.psum(
        (placed[0], placed[1], placed[2], placed[3], placed[4], placed[5], placed[6], placed[7]),
        ("ctx", "exp"),
    )
    return (
        block_out,
        tokens_grad,
        tables[0],
        tables[1],
        tables[2],
        tables[3],
        tables[4],
        tables[5],
        tables[6],
        tables[7],
        expert_tables[0],
        expert_tables[1],
        expert_tables[2],
        expert_tables[3],
        expert_tables[4],
        expert_tables[5],
    )


def solution(mesh):
    in_specs = (
        P("exp", "ctx", None),
        P("exp", "ctx", None),
        P(),
        P(),
        P(("ctx", "exp"), None),
        P(("ctx", "exp"), None),
        P(("ctx", "exp"), None),
        P(("ctx", "exp"), None),
        P("exp", None, None),
        P("exp", None, None),
        P("exp", None, None),
        P("exp", "ctx"),
        P("exp", "ctx", None),
        P("exp", "ctx", None),
        P(),
        P(),
        P(),
        P(),
        P(),
        P(),
        P(),
        P(),
        P(),
        P(None, "exp", None, None),
        P(None, "exp", None, None),
        P(None, "exp", None, None),
        P(None, "exp", None, None),
        P(None, "exp", None, None),
        P(None, "exp", None, None),
    )
    out_specs = (
        P("exp", "ctx", None),
        P("exp", "ctx", None),
        P(),
        P(),
        P(),
        P(),
        P(),
        P(),
        P(),
        P(),
        P(None, "exp", None, "ctx"),
        P(None, "exp", None, "ctx"),
        P(None, "exp", None, "ctx"),
        P(None, "exp", None, "ctx"),
        P(None, "exp", None, "ctx"),
        P(None, "exp", None, "ctx"),
    )
    return jax.shard_map(body, mesh=mesh, in_specs=in_specs, out_specs=out_specs, check_vma=False)
```

profile of v0, /device:TPU:0, one launch (start us, length us, event | category | flops | bytes accessed | tf_op | source)
XLA Modules:
  0.0 1765.0 jit_solution(5039217789717225150)
XLA Ops:
  15.4 53.3 %all-gather.14.cloned.1.call-done = bf16[1536,512]{1,0:T(8,128)(2,1)} async-done(((bf16[48,512]{1,0:T(8,128)(2,1)}), bf16[1536,512]{1,0:T(8,128)(2,1)}) %all-gather.14.cloned.1.call-update) | async-done | bytes 1572880 | tf_op jit(solution)/shard_map/all_gather | solution.py:222
  73.3 52.2 %all-gather.8.cloned.1.call-done = bf16[1536,512]{1,0:T(8,128)(2,1)} async-done(((bf16[48,512]{1,0:T(8,128)(2,1)}), bf16[1536,512]{1,0:T(8,128)(2,1)}) %all-gather.8.cloned.1.call-update) | async-done | bytes 1572880 | tf_op jit(solution)/shard_map/all_gather | solution.py:221
  130.9 11.3 reduce-window.6
  177.8 142.4 %all-gather.12.cloned.1.call-done = bf16[1536,1536]{1,0:T(8,128)(2,1)} async-done(((bf16[48,1536]{1,0:T(8,128)(2,1)}), bf16[1536,1536]{1,0:T(8,128)(2,1)}) %all-gather.12.cloned.1.call-update) | async-done | bytes 4718608 | tf_op jit(solution)/shard_map/all_gather | solution.py:220
  326.4 25.6 %while.31 = (s32[]{:T(128)}, f32[8,3,128]{2,1,0:T(4,128)}, f32[8,3,128]{2,1,0:T(4,128)}, f32[8,3,128,64]{2,3,1,0:T(8,128)S(1)}, s32[4]{0:T(128)}, /*index=5*/s32...) while((s32[]{:T(128)}, f32[8,3,128]{2,1,0:T(4,128)}, ...), condition=%wide.region_6.7_spmd, body=%wide.region_1.6_spmd.sunk | while | flops 212081664 | bytes 12409789 | solution.py:135
  354.6 30.7 %all-gather.18.cloned.1.call-done = bf16[1536,1536]{1,0:T(8,128)(2,1)} async-done(((bf16[48,1536]{1,0:T(8,128)(2,1)}), bf16[1536,1536]{1,0:T(8,128)(2,1)}) %all-gather.18.cloned.1.call-update) | async-done | bytes 4718608 | tf_op jit(solution)/shard_map/all_gather | solution.py:223
  441.7 94.5 %all-to-all-done = bf16[4,480,1536]{2,1,0:T(8,128)(2,1)} async-done(((bf16[4,480,1536]{2,1,0:T(8,128)(2,1)}), bf16[4,480,1536]{2,1,0:T(8,128)(2,1)}, u32[]{:S(2)}, u32[]{:S(2)}) %all-to-all-start) | async-done | bytes 5898272 | tf_op jit(solution)/shard_map/all_to_all | solution.py:289
  546.4 12.4 bitcast_add_fusion.4
  559.5 12.5 bitcast_add_fusion.3
  572.0 16.6 multiply_convert_fusion
  622.8 11.1 fusion.46
  633.9 11.1 fusion.42
  645.0 16.2 fusion.55
  666.9 76.5 %all-to-all-done.1 = bf16[4,480,1536]{2,1,0:T(8,128)(2,1)} async-done(((bf16[4,480,1536]{2,1,0:T(8,128)(2,1)}), bf16[4,480,1536]{2,1,0:T(8,128)(2,1)}, u32[]{:S(2)}, u32[]{:S(2)}) %all-to-all-start.1) | async-done | bytes 5898272 | tf_op jit(solution)/shard_map/all_to_all | solution.py:329
  760.5 117.5 %all-to-all-done.3 = bf16[4,480,1536]{2,1,0:T(8,128)(2,1)} async-done(((bf16[4,480,1536]{2,1,0:T(8,128)(2,1)}), bf16[4,480,1536]{2,1,0:T(8,128)(2,1)}, u32[]{:S(2)}, u32[]{:S(2)}) %all-to-all-start.3) | async-done | bytes 5898272 | tf_op jit(solution)/shard_map/all_to_all | solution.py:413
  904.9 23.6 %while.32 = (s32[]{:T(128)}, f32[8,3,128,64]{2,3,1,0:T(8,128)S(1)}, bf16[4,8,256,64]{2,3,1,0:T(8,128)(2,1)}, bf16[4,8,256,64]{2,3,1,0:T(8,128)(2,1)}, s32[4]{0:T...) while((s32[]{:T(128)}, f32[8,3,128,64]{2,3,1,0:T(8,128)S(1)}, ...), condition=%wide.region_20.23_spmd, body=%wide.region_17.22_spmd.sunk | while | flops 511968256 | bytes 21425072 | solution.py:499
  943.3 14.3 copy.199
  957.5 31.0 %reshape.407 = bf16[512,1280]{1,0:T(8,128)(2,1)} reshape(bf16[512,10,16,8]{3,2,1,0:T(8,128)(2,1)} %bitcast.396) | data formatting | bytes 2621440
  991.6 14.3 copy.193
  1005.9 31.0 %reshape.401 = bf16[512,1280]{1,0:T(8,128)(2,1)} reshape(bf16[512,10,16,8]{3,2,1,0:T(8,128)(2,1)} %bitcast.397) | data formatting | bytes 2621440
  1039.7 14.3 copy.197
  1054.0 30.9 %reshape.405 = bf16[512,1280]{1,0:T(8,128)(2,1)} reshape(bf16[512,10,16,8]{3,2,1,0:T(8,128)(2,1)} %bitcast.398) | data formatting | bytes 2621440
  1096.2 44.3 %copy.195 = bf16[8,10,16,1536]{0,2,1,3:T(8,128)(2,1)} copy(bf16[8,10,16,1536]{3,0,2,1:T(8,128)(2,1)} %convolution_convert_fusion.1) | data formatting | bytes 7864320
  1140.5 88.7 %reshape.403 = bf16[1536,1280]{1,0:T(8,128)(2,1)} reshape(bf16[1536,10,16,8]{3,2,1,0:T(8,128)(2,1)} %bitcast.392) | data formatting | bytes 7864320
  1241.2 44.4 %copy.191 = bf16[8,10,16,1536]{0,2,1,3:T(8,128)(2,1)} copy(bf16[8,10,16,1536]{3,0,2,1:T(8,128)(2,1)} %convolution_convert_fusion.2) | data formatting | bytes 7864320
  1285.5 88.6 %reshape.399 = bf16[1536,1280]{1,0:T(8,128)(2,1)} reshape(bf16[1536,10,16,8]{3,2,1,0:T(8,128)(2,1)} %bitcast.393) | data formatting | bytes 7864320
  1386.1 44.3 %copy.201 = bf16[8,10,16,1536]{0,2,1,3:T(8,128)(2,1)} copy(bf16[8,10,16,1536]{3,0,2,1:T(8,128)(2,1)} %convolution_convert_fusion) | data formatting | bytes 7864320
  1430.5 88.6 %reshape.409 = bf16[1536,1280]{1,0:T(8,128)(2,1)} reshape(bf16[1536,10,16,8]{3,2,1,0:T(8,128)(2,1)} %bitcast.394) | data formatting | bytes 7864320
  1557.6 11.4 reshape.404
  1578.3 11.4 reshape.400
  1598.9 11.4 reshape.410
  1630.1 118.9 %all-reduce.3.cloned.1.call-done = (f32[8,16,1536]{2,1,0:T(8,128)}, f32[8,16,1536]{2,1,0:T(8,128)}, f32[8,16,1536]{2,1,0:T(8,128)}, f32[8,16,512]{2,1,0:T(8,128)...) async-done(((f32[8,16,1536]{2,1,0:T(8,128)}, f32[8,16,1536]{2,1,0:T(8,128)}, f32[8,16,1536]{2,1,0:T(8,128)}, ...) | async-done | bytes 5242896 | tf_op jit(solution)/shard_map/psum | solution.py:571
  (427 shorter events, 407.0 us)
Async XLA Ops:
  7.2 399.2 %copy-start = (bf16[8,10,16,512]{3,2,1,0:T(8,128)(2,1)S(1)}, bf16[8,10,16,512]{3,2,1,0:T(8,128)(2,1)}, u32[]{:S(2)}) copy-start(bf16[8,10,16,512]{3,2,1,0:T(8,128)(2,1)} %param.68) | copy-start | bytes 3932164
  7.2 65.0 %copy-start.12 = (bf16[1,128,1536]{2,1,0:T(8,128)(2,1)S(1)}, bf16[1,128,1536]{2,1,0:T(8,128)(2,1)}, u32[]{:S(2)}) copy-start(bf16[1,128,1536]{2,1,0:T(8,128)(2,1)} %param.41) | copy-start | bytes 1179652
  7.2 65.0 %copy-start.63 = (f32[1536]{0:T(1024)S(1)}, f32[1536]{0:T(1024)}, u32[]{:S(2)}) copy-start(f32[1536]{0:T(1024)} %param.43) | copy-start | bytes 18436
  7.2 61.5 %all-gather.14.cloned.1.call-start = ((), (), s32[]{:S(2)}) async-start(), calls=%async_computation.15 | async-start | bytes 1622016 | tf_op jit(solution)/shard_map/all_gather | solution.py:222
  8.0 117.6 %all-gather.8.cloned.1.call-start = ((), (), s32[]{:S(2)}) async-start(), calls=%async_computation.12 | async-start | bytes 1622016 | tf_op jit(solution)/shard_map/all_gather | solution.py:221
  8.7 160.4 %all-gather.16.cloned.1.call-start = ((), (), s32[]{:S(2)}) async-start(), calls=%async_computation.16 | async-start | bytes 1179648 | tf_op jit(solution)/shard_map/all_gather | solution.py:261
  12.9 155.1 %copy-start.81 = (f32[128]{0:T(128)}, f32[128]{0:T(128)S(1)}, u32[]{:S(2)}) copy-start(f32[128]{0:T(128)S(1)} %add_rsqrt_fusion.1) | copy-start | bytes 1540
  14.2 113.1 %copy-start.72 = (bf16[128,16]{0,1:T(8,128)(2,1)}, bf16[128,16]{0,1:T(8,128)(2,1)S(1)}, u32[]{:S(2)}) copy-start(bf16[128,16]{0,1:T(8,128)(2,1)S(1)} %convolution_convert_fusion.9) | copy-start | bytes 12292
  15.4 304.8 %copy-start.6 = (bf16[128,1536]{1,0:T(8,128)(2,1)}, bf16[128,1536]{1,0:T(8,128)(2,1)S(1)}, u32[]{:S(2)}) copy-start(bf16[128,1536]{1,0:T(8,128)(2,1)S(1)} %fusion.149) | copy-start | bytes 1179652
  15.4 114.7 %copy-start.76 = (s32[1,128,8]{1,2,0:T(8,128)S(1)}, s32[1,128,8]{1,2,0:T(8,128)}, u32[]{:S(2)}) copy-start(s32[1,128,8]{1,2,0:T(8,128)} %param.53) | copy-start | bytes 12292
  15.4 115.2 %copy-start.70 = (f32[1,128,8]{1,2,0:T(8,128)S(1)}, f32[1,128,8]{1,2,0:T(8,128)}, u32[]{:S(2)}) copy-start(f32[1,128,8]{1,2,0:T(8,128)} %param.54) | copy-start | bytes 12292
  70.5 72.2 %copy-start.31 = (bf16[1,128,1536]{2,1,0:T(8,128)(2,1)S(1)}, bf16[1,128,1536]{2,1,0:T(8,128)(2,1)}, u32[]{:S(2)}) copy-start(bf16[1,128,1536]{2,1,0:T(8,128)(2,1)} %param.42) | copy-start | bytes 1179652
  72.2 104.1 %all-gather.10.cloned.1.call-start = ((), (), s32[]{:S(2)}) async-start(), calls=%async_computation.13 | async-start | bytes 1179648 | tf_op jit(solution)/shard_map/all_gather | solution.py:260
  73.3 57.4 %copy-start.74 = (bf16[128,16]{0,1:T(8,128)(2,1)}, bf16[128,16]{0,1:T(8,128)(2,1)S(1)}, u32[]{:S(2)}) copy-start(bf16[128,16]{0,1:T(8,128)(2,1)S(1)} %convolution_convert_fusion.11) | copy-start | bytes 12292
  129.0 191.2 %all-gather.12.cloned.1.call-start = ((), (), s32[]{:S(2)}) async-start(), calls=%async_computation.14 | async-start | bytes 4866048 | tf_op jit(solution)/shard_map/all_gather | solution.py:220
  129.6 255.8 %all-gather.18.cloned.1.call-start = ((), (), s32[]{:S(2)}) async-start(), calls=%async_computation.17 | async-start | bytes 4866048 | tf_op jit(solution)/shard_map/all_gather | solution.py:223
  152.2 248.1 %all-to-all-start.2 = ((bf16[4,480,1536]{2,1,0:T(8,128)(2,1)}), bf16[4,480,1536]{2,1,0:T(8,128)(2,1)}, u32[]{:S(2)}, u32[]{:S(2)}) async-start(bf16[4,480,1536]{2,1,0:T(8,128)(2,1)} %bitcast.403), calls=%async_computation.2 | async-start | bytes 11796480 | tf_op jit(solution)/shard_map/all_to_all | solution.py:348
  169.1 154.2 %copy-start.67 = (bf16[128,16]{0,1:T(8,128)(2,1)}, bf16[128,16]{0,1:T(8,128)(2,1)S(1)}, u32[]{:S(2)}) copy-start(bf16[128,16]{0,1:T(8,128)(2,1)S(1)} %convolution_convert_fusion.10) | copy-start | bytes 12292
  354.6 35.5 %copy-start.58 = (f32[1536]{0:T(1024)S(1)}, f32[1536]{0:T(1024)}, u32[]{:S(2)}) copy-start(f32[1536]{0:T(1024)} %param.44) | copy-start | bytes 18436
  354.6 36.4 %copy-start.78 = (s32[1024,1]{0,1:T(1,128)S(1)}, s32[1024,1]{0,1:T(1,128)}, u32[]{:S(2)}) copy-start(s32[1024,1]{0,1:T(1,128)} %copy-done.77) | copy-start | bytes 12292
  400.3 135.9 %all-to-all-start = ((bf16[4,480,1536]{2,1,0:T(8,128)(2,1)}), bf16[4,480,1536]{2,1,0:T(8,128)(2,1)}, u32[]{:S(2)}, u32[]{:S(2)}) async-start(bf16[4,480,1536]{2,1,0:T(8,128)(2,1)} %bitcast.404), calls=%async_computation | async-start | bytes 11796480 | tf_op jit(solution)/shard_map/all_to_all | solution.py:289
  608.4 135.0 %all-to-all-start.1 = ((bf16[4,480,1536]{2,1,0:T(8,128)(2,1)}), bf16[4,480,1536]{2,1,0:T(8,128)(2,1)}, u32[]{:S(2)}, u32[]{:S(2)}) async-start(bf16[4,480,1536]{2,1,0:T(8,128)(2,1)} %bitcast.406), calls=%async_computation.1 | async-start | bytes 11796480 | tf_op jit(solution)/shard_map/all_to_all | solution.py:329
  743.4 134.6 %all-to-all-start.3 = ((bf16[4,480,1536]{2,1,0:T(8,128)(2,1)}), bf16[4,480,1536]{2,1,0:T(8,128)(2,1)}, u32[]{:S(2)}, u32[]{:S(2)}) async-start(bf16[4,480,1536]{2,1,0:T(8,128)(2,1)} %bitcast.405), calls=%async_computation.3 | async-start | bytes 11796480 | tf_op jit(solution)/shard_map/all_to_all | solution.py:413
  748.8 773.3 %reduce-scatter.27.cloned.1.call-start = ((), (), s32[]{:S(2)}) async-start(), calls=%async_computation.19 | async-start | bytes 1179648
  933.1 590.1 %reduce-scatter.25.cloned.1.call-start = ((), (), s32[]{:S(2)}) async-start(), calls=%async_computation.18 | async-start | bytes 1179648
  940.4 589.5 %reduce-scatter.37.cloned.1.call-start = ((), (), s32[]{:S(2)}) async-start(), calls=%async_computation.24 | async-start | bytes 1474560
  988.6 550.6 %reduce-scatter.31.cloned.1.call-start = ((), (), s32[]{:S(2)}) async-start(), calls=%async_computation.21 | async-start | bytes 1474560
  1036.9 511.5 %reduce-scatter.35.cloned.1.call-start = ((), (), s32[]{:S(2)}) async-start(), calls=%async_computation.23 | async-start | bytes 1474560
  1084.9 472.7 %reduce-scatter.33.cloned.1.call-start = ((), (), s32[]{:S(2)}) async-start(), calls=%async_computation.22 | async-start | bytes 4423680
  1229.2 349.1 %reduce-scatter.29.cloned.1.call-start = ((), (), s32[]{:S(2)}) async-start(), calls=%async_computation.20 | async-start | bytes 4423680
  1374.2 224.7 %reduce-scatter.39.cloned.1.call-start = ((), (), s32[]{:S(2)}) async-start(), calls=%async_computation.25 | async-start | bytes 4423680
  1519.2 229.8 %all-reduce.3.cloned.1.call-start = ((), (), s32[]{:S(2)}) async-start(), calls=%async_computation.26 | async-start | bytes 10485760 | tf_op jit(solution)/shard_map/psum | solution.py:571
  (71 other events, 558.7 us)
Sparse Core Ops, SparseCore 0:
  10.9 57.7 all-gather.13
  71.6 53.9 all-gather.7
  128.0 22.3 all-gather.15
  152.8 23.4 all-gather.9
  178.9 141.1 all-gather.11
  322.8 62.4 all-gather.17
  933.2 56.2 reduce-scatter.26
  992.7 36.0 reduce-scatter.24
  1032.5 37.2 reduce-scatter.36
  1073.5 37.3 reduce-scatter.30
  1114.7 37.3 reduce-scatter.34
  1229.3 70.2 reduce-scatter.32
  1374.3 70.2 reduce-scatter.28
  1519.3 70.2 reduce-scatter.38
  1598.1 150.7 all-reduce.2
where the time goes:
time: 1780 us; the launch traced here: 1770 us
  local copies, waits for them, and re-layouts  745 us (42%)
  waiting for transfers between devices  693 us (39%)
  matrix products  212 us (12%)
  other arithmetic  53.6 us (3%)
  starting transfers between devices  23.2 us (1%)
    unnamed x202, local copies, waits for them, and re-layouts  650 us
    all_gather x1, waiting for transfers between devices, body(): lax.all_gather(w_query, ('ctx', 'exp'), axis=0, tiled=True)  142 us
    psum x1, waiting for transfers between devices, body(): lax.psum((placed[0], placed[1], placed[2], placed[3], placed[4], placed[5...  119 us
    all_to_all x1, waiting for transfers between devices, body(): lax.all_to_all(grad_received.astype(jnp.bfloat16).reshape(exp_size, local...  117 us
    all_to_all x1, waiting for transfers between devices, body(): lax.all_to_all(scatter_rows(jnp.repeat(normed_mid, TOPK, axis=0)), 'exp',...  94.5 us
    all_to_all x1, waiting for transfers between devices, body(): lax.all_to_all(specialist_answer.astype(jnp.bfloat16).reshape(exp_size, l...  76.5 us
    all_gather x1, waiting for transfers between devices, body(): lax.all_gather(content_projection, ('ctx', 'exp'), axis=0, tiled=True)  53.3 us
    all_gather x1, waiting for transfers between devices, body(): lax.all_gather(lock_projection, ('ctx', 'exp'), axis=0, tiled=True)  52.2 us
  transfers between devices with their start and end apart: 19, of which 9 were waited for; matrix products, arithmetic and copies ran while one was open for 50% of the time, Pallas kernels for 0%

commit v1 on v0

v1 whole, which is shorter than its diff:
```python
import functools

import jax
import jax.numpy as jnp
from jax import lax
from jax.experimental import pallas as pl
from jax.experimental.pallas import tpu as pltpu
from jax.sharding import PartitionSpec as P

ASKING_ATTENDERS = 24
PAIRED_ATTENDERS = 8
ATTENTION_EXTENT = 64
HEADS_PER_PAIR = ASKING_ATTENDERS // PAIRED_ATTENDERS
QUERY_COLS = HEADS_PER_PAIR * ATTENTION_EXTENT
EXPERTS = 40
TOPK = 8
NUM_CHOICES_X = 8
CAP = 48
RANK = 16
LANES = 128

EPS = 1e-06
LOW_FACTORED = 2.0
MASKED_FLOOR = -1e30
SCALE = 0.125
VMEM_LIMIT = 56 * 1024 * 1024

bf16 = jnp.bfloat16
f32 = jnp.float32

HEAD_COLS = 384


def nn(left, right):
    return jnp.dot(left, right, preferred_element_type=f32)


def nt(left, right):
    return lax.dot_general(left, right, (((1,), (1,)), ((), ())), preferred_element_type=f32)


def tn(left, right):
    return lax.dot_general(left, right, (((0,), (0,)), ((), ())), preferred_element_type=f32)


def normed(rows, gain):
    factor = lax.rsqrt(jnp.mean(rows * rows, axis=-1, keepdims=True) + EPS)
    return rows * factor * gain, factor


def norm_back(rows, factor, gain, adjoint):
    weighted = adjoint * gain
    central = jnp.mean(weighted * rows, axis=-1, keepdims=True)
    return factor * (weighted - rows * factor * factor * central)


def whole_block(shape):
    return pl.BlockSpec(shape, lambda *ids: (0,) * len(shape))


def call_params(axes=1):
    return pltpu.CompilerParams(
        dimension_semantics=("arbitrary",) * axes, vmem_limit_bytes=VMEM_LIMIT
    )


def key_mask(seg_col, seg_row, tile, start, kmax):
    key_place = lax.broadcasted_iota(jnp.int32, (kmax, tile), 0)
    query_place = start + lax.broadcasted_iota(jnp.int32, (kmax, tile), 1)
    key_seg = seg_col[pl.ds(0, kmax), :]
    query_seg = seg_row[:, pl.ds(start, tile)]
    same = (key_seg == query_seg) | (key_seg == 0.0)
    return (key_place <= query_place) & same


def project_attend_kernel(
    blocks, ways, order_ref, x_ref, w_ref, first_ref, second_ref, seg_col, seg_row,
    qkv_ref, inner_ref, att_ref, lse_ref, turned,
):
    step = pl.program_id(0)
    rows = x_ref.shape[1]
    x = x_ref[0]
    inner = nt(x, first_ref[...]).astype(bf16)
    qkv = (nn(x, w_ref[...]) + LOW_FACTORED * nn(inner, second_ref[...])).astype(bf16)
    here = pl.ds(pl.multiple_of(step * rows, rows), rows)
    qkv_ref[here, :] = qkv
    inner_ref[here, :] = inner
    turned[:, here] = qkv.astype(f32).T.astype(bf16)

    @pl.when(step == blocks - 1)
    def _():
        part = order_ref[blocks]
        if ways > 1:
            att_ref[...] = jnp.zeros_like(att_ref)
            lse_ref[...] = jnp.zeros_like(lse_ref)
        per_tile = 2 if ways == 1 else 1
        tile = per_tile * rows
        for index in range(blocks // ways // per_tile):
            kmax = (index + 1) * per_tile * ways * rows
            start = pl.multiple_of((index * per_tile * ways + part) * rows, rows)
            if ways == 1:
                start = index * tile
            allowed = key_mask(seg_col, seg_row, tile, start, kmax)
            keys = qkv_ref[pl.ds(0, kmax), 0:LANES]
            values_t = turned[ATTENTION_EXTENT:LANES, pl.ds(0, kmax)]
            outs = []
            sums = []
            for head in range(HEADS_PER_PAIR):
                base = LANES + head * ATTENTION_EXTENT
                q_t = turned[base : base + ATTENTION_EXTENT, pl.ds(start, tile)] * SCALE
                q_pad = jnp.concatenate([q_t, jnp.zeros_like(q_t)], axis=0)
                score = jnp.where(allowed, nn(keys, q_pad), MASKED_FLOOR)
                top = jnp.max(score, axis=0, keepdims=True)
                weight = jnp.exp(score - top)
                total = jnp.sum(weight, axis=0, keepdims=True)
                prob = (weight * (1.0 / total)).astype(bf16)
                outs.append(nn(values_t, prob))
                sums.append(top + jnp.log(total))
            packed = jnp.concatenate(outs, axis=0)
            att_ref[pl.ds(start, tile), :] = packed.T.astype(bf16)
            lse_ref[:, pl.ds(start, tile)] = jnp.concatenate(
                sums + [jnp.zeros((8 - HEADS_PER_PAIR, tile), f32)], axis=0
            )


def project_attend(order, x_blocks, weights, first, second, seg_col, seg_row, ways):
    blocks, rows, width = x_blocks.shape
    total = blocks * rows
    return pl.pallas_call(
        functools.partial(project_attend_kernel, blocks, ways),
        grid_spec=pltpu.PrefetchScalarGridSpec(
            num_scalar_prefetch=1,
            grid=(blocks,),
            in_specs=[
                pl.BlockSpec((1, rows, width), lambda i, order: (order[i], 0, 0)),
                whole_block(weights.shape),
                whole_block(first.shape),
                whole_block(second.shape),
                whole_block(seg_col.shape),
                whole_block(seg_row.shape),
            ],
            out_specs=[
                whole_block((total, HEAD_COLS)),
                whole_block((total, LANES)),
                whole_block((total, QUERY_COLS)),
                whole_block((8, total)),
            ],
            scratch_shapes=[pltpu.VMEM((HEAD_COLS, total), bf16)],
        ),
        out_shape=[
            jax.ShapeDtypeStruct((total, HEAD_COLS), bf16),
            jax.ShapeDtypeStruct((total, LANES), bf16),
            jax.ShapeDtypeStruct((total, QUERY_COLS), bf16),
            jax.ShapeDtypeStruct((8, total), f32),
        ],
        compiler_params=call_params(),
        cost_estimate=pl.CostEstimate(
            flops=2 * total * width * 512 + 8 * total * total * 256,
            bytes_accessed=2 * total * width * 2,
            transcendentals=HEADS_PER_PAIR * total * total,
        ),
        name="project_attend",
    )(order, x_blocks, weights, first, second, seg_col, seg_row)


def attend_back_kernel(
    blocks, ways, order_ref, qkv_ref, adj_ref, lse_ref, second_ref, inner_ref, seg_col, seg_row,
    grad_ref, grad_inner_ref, grad_second_ref, turned, adj_turned, grad_kv,
):
    total = qkv_ref.shape[0]
    rows = total // blocks
    part = order_ref[blocks]
    half = ATTENTION_EXTENT
    for index in range(blocks):
        here = pl.ds(index * rows, rows)
        turned[:, here] = qkv_ref[here, :].astype(f32).T.astype(bf16)
        adj_turned[:, here] = adj_ref[here, :].astype(f32).T.astype(bf16)
    grad_kv[...] = jnp.zeros_like(grad_kv)
    if ways > 1:
        grad_ref[...] = jnp.zeros_like(grad_ref)
    per_tile = 2 if ways == 1 else 1
    tile = per_tile * rows
    zero = jnp.zeros((half, tile), bf16)
    for index in range(blocks // ways // per_tile):
        kmax = (index + 1) * per_tile * ways * rows
        start = pl.multiple_of((index * per_tile * ways + part) * rows, rows)
        if ways == 1:
            start = index * tile
        allowed = key_mask(seg_col, seg_row, tile, start, kmax)
        keys = qkv_ref[pl.ds(0, kmax), 0:LANES]
        keys_t = turned[0:half, pl.ds(0, kmax)]
        grads_q = []
        update = jnp.zeros((kmax, LANES), f32)
        for head in range(HEADS_PER_PAIR):
            base = LANES + head * half
            q_t = turned[base : base + half, pl.ds(start, tile)] * SCALE
            q_pad = jnp.concatenate([q_t, zero], axis=0)
            a_t = adj_turned[head * half : (head + 1) * half, pl.ds(start, tile)]
            a_pad = jnp.concatenate([zero, a_t], axis=0)
            score = nn(keys, q_pad) - lse_ref[head : head + 1, pl.ds(start, tile)]
            prob = jnp.where(allowed, jnp.exp(jnp.where(allowed, score, 0.0)), 0.0)
            grad_prob = nn(keys, a_pad)
            both = prob * grad_prob
            delta = jnp.sum(both, axis=0, keepdims=True)
            grad_score = (both - prob * delta).astype(bf16)
            update = update + nt(grad_score, q_pad) + nt(prob.astype(bf16), a_pad)
            grads_q.append(nn(keys_t, grad_score) * SCALE)
        grad_kv[pl.ds(0, kmax), :] += update
        packed = jnp.concatenate(grads_q + [jnp.zeros((half, tile), f32)], axis=0)
        grad_ref[pl.ds(start, tile), LANES:] = packed.T.astype(bf16)
    grad_ref[:, 0:LANES] = grad_kv[...].astype(bf16)
    grad = grad_ref[...]
    grad_inner_ref[...] = (LOW_FACTORED * nt(grad, second_ref[...])).astype(bf16)
    grad_second_ref[...] = LOW_FACTORED * tn(inner_ref[...], grad)


def attend_back(order, qkv, adj, lse, second, inner, seg_col, seg_row, blocks, ways):
    total = qkv.shape[0]
    return pl.pallas_call(
        functools.partial(attend_back_kernel, blocks, ways),
        grid_spec=pltpu.PrefetchScalarGridSpec(
            num_scalar_prefetch=1,
            grid=(1,),
            in_specs=[
                whole_block(v.shape) for v in (qkv, adj, lse, second, inner, seg_col, seg_row)
            ],
            out_specs=[
                whole_block((total, HEAD_COLS)),
                whole_block((total, LANES)),
                whole_block((LANES, HEAD_COLS)),
            ],
            scratch_shapes=[
                pltpu.VMEM((HEAD_COLS, total), bf16),
                pltpu.VMEM((QUERY_COLS, total), bf16),
                pltpu.VMEM((total, LANES), f32),
            ],
        ),
        out_shape=[
            jax.ShapeDtypeStruct((total, HEAD_COLS), bf16),
            jax.ShapeDtypeStruct((total, LANES), bf16),
            jax.ShapeDtypeStruct((LANES, HEAD_COLS), f32),
        ],
        compiler_params=call_params(),
        cost_estimate=pl.CostEstimate(
            flops=20 * total * total * 256,
            bytes_accessed=total * 2000,
            transcendentals=HEADS_PER_PAIR * total * total,
        ),
        name="attend_back",
    )(order, qkv, adj, lse, second, inner, seg_col, seg_row)


def first_grad_kernel(order_ref, x_ref, grad_inner_ref, out_ref):
    @pl.when(pl.program_id(0) == 0)
    def _():
        out_ref[...] = jnp.zeros_like(out_ref)

    out_ref[...] += tn(grad_inner_ref[...], x_ref[0])


def first_grad(order, x_blocks, grad_inner):
    blocks, rows, width = x_blocks.shape
    return pl.pallas_call(
        first_grad_kernel,
        grid_spec=pltpu.PrefetchScalarGridSpec(
            num_scalar_prefetch=1,
            grid=(blocks,),
            in_specs=[
                pl.BlockSpec((1, rows, width), lambda i, order: (order[i], 0, 0)),
                pl.BlockSpec((rows, LANES), lambda i, order: (i, 0)),
            ],
            out_specs=whole_block((LANES, width)),
        ),
        out_shape=jax.ShapeDtypeStruct((LANES, width), f32),
        compiler_params=call_params(),
        cost_estimate=pl.CostEstimate(
            flops=2 * blocks * rows * width * LANES,
            bytes_accessed=blocks * rows * width * 2,
            transcendentals=0,
        ),
        name="first_grad",
    )(order, x_blocks, grad_inner)


def source_mask(shape, sources):
    row = lax.broadcasted_iota(jnp.int32, shape, 0)
    col = lax.broadcasted_iota(jnp.int32, shape, 1)
    keep = None
    for source in range(sources):
        inside = (row >= source * CAP) & (row < (source + 1) * CAP)
        inside &= (lax.rem(col, sources * RANK) >= source * RANK) & (
            lax.rem(col, sources * RANK) < (source + 1) * RANK
        )
        keep = inside if keep is None else keep | inside
    return keep


def masked(values, sources):
    return jnp.where(source_mask(values.shape, sources), values, 0.0)


def picks(slot_ref, pair, tokens):
    slots = slot_ref[0, :, pair * 2 * tokens : (pair + 1) * 2 * tokens]
    place = lax.broadcasted_iota(jnp.int32, (2 * CAP, 2 * tokens), 0)
    return place == slots


def picked_rows(slot_ref, rows_ref, sources):
    tokens = rows_ref.shape[0] // sources
    parts = []
    for pair in range(sources // 2):
        pick = picks(slot_ref, pair, tokens).astype(f32).astype(bf16)
        rows = rows_ref[pair * 2 * tokens : (pair + 1) * 2 * tokens, :]
        parts.append(nn(pick, rows))
    return jnp.concatenate(parts, axis=0)


def picked_gates(slot_ref, gate_ref, sources):
    tokens = gate_ref.shape[2] // sources
    parts = []
    for pair in range(sources // 2):
        gate = gate_ref[0, :, pair * 2 * tokens : (pair + 1) * 2 * tokens]
        kept = jnp.where(picks(slot_ref, pair, tokens), gate, 0.0)
        parts.append(jnp.sum(kept, axis=1, keepdims=True))
    return jnp.concatenate(parts, axis=0)


def combine(target_ref, values, out_ref, sources):
    tokens = target_ref.shape[0] // sources
    slots = values.shape[1]
    for source in range(sources):
        target = target_ref[source * tokens : (source + 1) * tokens, :]
        place = lax.broadcasted_iota(jnp.int32, (tokens, slots), 1)
        hit = place == target[:, 0:1]
        for choice in range(1, TOPK):
            hit |= place == target[:, choice : choice + 1]
        out_ref[source] = nn(hit.astype(f32).astype(bf16), values[source]).astype(bf16)


def keep_rows(values, rows, expert, sources):
    for source in range(sources):
        values[source, pl.ds(pl.multiple_of(expert * CAP, CAP), CAP), :] = rows[
            source * CAP : (source + 1) * CAP
        ]


def experts_pre_kernel(
    sources, slot_ref, gate_ref, grads_ref, down_ref, down_first, down_second,
    picked_ref, hidden_ref, inner_ref,
):
    grads = picked_rows(slot_ref, grads_ref, sources)
    grads = (grads * picked_gates(slot_ref, gate_ref, sources)).astype(bf16)
    picked_ref[0] = grads
    inner = LOW_FACTORED * nt(grads, down_second[0])
    inner = masked(inner, sources).astype(bf16)
    inner_ref[0] = inner
    hidden_ref[0] = nt(grads, down_ref[0]) + nn(inner, down_first[0])


def experts_main_kernel(
    sources, slot_ref, x_ref, firsts, seconds, gate_w, up_w, grad_hidden, target_ref,
    picked_ref, hidden_ref, adj_ref, inner_ref, out_ref, values,
):
    expert = pl.program_id(0)
    inner_size = gate_w.shape[2]
    x = picked_rows(slot_ref, x_ref, sources).astype(bf16)
    picked_ref[0] = x
    inner = masked(nt(x, firsts[0]), sources).astype(bf16)
    added = LOW_FACTORED * nn(inner, seconds[0])
    gate = nn(x, gate_w[0]) + added[:, :inner_size]
    up = nn(x, up_w[0]) + added[:, inner_size:]
    sigma = 1.0 / (1.0 + jnp.exp(-gate))
    active = gate * sigma
    hidden_ref[0] = (active * up).astype(bf16)
    adj = grad_hidden[0]
    grad_gate = (adj * up * sigma * (1.0 + gate * (1.0 - sigma))).astype(bf16)
    grad_up = (adj * active).astype(bf16)
    both = jnp.concatenate([grad_gate, grad_up], axis=1)
    adj_ref[0] = both
    grad_inner = masked(LOW_FACTORED * nt(both, seconds[0]), sources).astype(bf16)
    inner_ref[0] = jnp.concatenate([inner, grad_inner], axis=1)
    rows = nt(grad_gate, gate_w[0]) + nt(grad_up, up_w[0]) + nn(grad_inner, firsts[0])
    keep_rows(values, rows.astype(bf16), expert, sources)

    @pl.when(expert == pl.num_programs(0) - 1)
    def _():
        combine(target_ref, values, out_ref, sources)


def experts_post_kernel(
    sources, cohort, slot_ref, gate_ref, down_ref, down_first, down_second, picked_ref, hidden_ref,
    adj_ref, inner_ref, picked_grads, grad_inner_down, target_ref,
    table_ref, out_ref, values,
):
    expert = pl.program_id(0)
    span = sources * RANK
    hidden = hidden_ref[0]
    inner_down = masked(nt(hidden, down_first[0]), sources).astype(bf16)
    answer = nn(hidden, down_ref[0]) + LOW_FACTORED * nn(inner_down, down_second[0])
    answer = answer.astype(bf16).astype(f32) * picked_gates(slot_ref, gate_ref, sources)
    keep_rows(values, answer.astype(bf16), expert, sources)
    width = picked_ref.shape[2]
    inner_size = hidden.shape[1]
    inner = inner_ref[0, :, : 2 * span]
    grad_inner = inner_ref[0, :, 2 * span :]
    firsts = tn(grad_inner, picked_ref[0])
    seconds = LOW_FACTORED * tn(inner, adj_ref[0])
    down_firsts = tn(grad_inner_down[0], hidden)
    down_seconds = LOW_FACTORED * tn(inner_down, picked_grads[0])
    wide, slim = width // cohort, inner_size // cohort
    wide_parts = (firsts[:span], firsts[span:], down_seconds)
    slim_parts = (seconds[:span, :inner_size], seconds[span:, inner_size:], down_firsts)
    for place in range(cohort):
        pieces = [v[:, place * wide : (place + 1) * wide] for v in wide_parts]
        pieces += [v[:, place * slim : (place + 1) * slim] for v in slim_parts]
        table_ref[place, 0] = jnp.concatenate(pieces, axis=1).astype(bf16)

    @pl.when(expert == pl.num_programs(0) - 1)
    def _():
        combine(target_ref, values, out_ref, sources)


def per_expert(array):
    rest = array.shape[1:]
    return pl.BlockSpec((1,) + rest, lambda e: (e,) + (0,) * len(rest))


def experts_pre(slots, gates, grads, down, down_first, down_second):
    experts, sources = slots.shape[0], down_first.shape[1] // RANK
    width, inner_size = down.shape[2], down.shape[1]
    rows = sources * CAP
    return pl.pallas_call(
        functools.partial(experts_pre_kernel, sources),
        grid=(experts,),
        in_specs=[
            per_expert(slots),
            per_expert(gates),
            whole_block((grads.shape[0], width)),
            per_expert(down),
            per_expert(down_first),
            per_expert(down_second),
        ],
        out_specs=[
            pl.BlockSpec((1, rows, width), lambda e: (e, 0, 0)),
            pl.BlockSpec((1, rows, inner_size), lambda e: (e, 0, 0)),
            pl.BlockSpec((1, rows, sources * RANK), lambda e: (e, 0, 0)),
        ],
        out_shape=[
            jax.ShapeDtypeStruct((experts, rows, width), bf16),
            jax.ShapeDtypeStruct((experts, rows, inner_size), f32),
            jax.ShapeDtypeStruct((experts, rows, sources * RANK), bf16),
        ],
        compiler_params=call_params(),
        cost_estimate=pl.CostEstimate(
            flops=2 * experts * rows * width * inner_size * 2,
            bytes_accessed=experts * width * (inner_size * 2 + rows * 2),
            transcendentals=0,
        ),
        name="experts_pre",
    )(slots, gates, grads, down, down_first, down_second)


def experts_main(slots, x, firsts, seconds, gate_w, up_w, grad_hidden, target):
    experts, width, inner_size = gate_w.shape
    sources = firsts.shape[1] // (2 * RANK)
    rows = sources * CAP
    tokens = x.shape[0] // sources
    return pl.pallas_call(
        functools.partial(experts_main_kernel, sources),
        grid=(experts,),
        in_specs=[
            per_expert(slots),
            whole_block(x.shape),
            per_expert(firsts),
            per_expert(seconds),
            per_expert(gate_w),
            per_expert(up_w),
            per_expert(grad_hidden),
            whole_block(target.shape),
        ],
        out_specs=[
            pl.BlockSpec((1, rows, width), lambda e: (e, 0, 0)),
            pl.BlockSpec((1, rows, inner_size), lambda e: (e, 0, 0)),
            pl.BlockSpec((1, rows, 2 * inner_size), lambda e: (e, 0, 0)),
            pl.BlockSpec((1, rows, 4 * sources * RANK), lambda e: (e, 0, 0)),
            whole_block((sources, tokens, width)),
        ],
        out_shape=[
            jax.ShapeDtypeStruct((experts, rows, width), bf16),
            jax.ShapeDtypeStruct((experts, rows, inner_size), bf16),
            jax.ShapeDtypeStruct((experts, rows, 2 * inner_size), bf16),
            jax.ShapeDtypeStruct((experts, rows, 4 * sources * RANK), bf16),
            jax.ShapeDtypeStruct((sources, tokens, width), bf16),
        ],
        scratch_shapes=[pltpu.VMEM((sources, experts * CAP, width), bf16)],
        compiler_params=call_params(),
        cost_estimate=pl.CostEstimate(
            flops=2 * experts * rows * width * inner_size * 5,
            bytes_accessed=experts * width * (inner_size * 4 + rows * 4),
            transcendentals=experts * rows * inner_size,
        ),
        name="experts_main",
    )(slots, x, firsts, seconds, gate_w, up_w, grad_hidden, target)


def experts_post(
    slots, gates, down, down_first, down_second, picked, hidden, adj, inner, picked_grads,
    grad_inner_down, target, cohort,
):
    experts, inner_size, width = down.shape
    sources = down_first.shape[1] // RANK
    rows = sources * CAP
    tokens = target.shape[0] // sources
    lanes = 3 * (width + inner_size) // cohort
    return pl.pallas_call(
        functools.partial(experts_post_kernel, sources, cohort),
        grid=(experts,),
        in_specs=[
            per_expert(v)
            for v in (
                slots, gates, down, down_first, down_second, picked, hidden, adj, inner,
                picked_grads, grad_inner_down,
            )
        ]
        + [whole_block(target.shape)],
        out_specs=[
            pl.BlockSpec((cohort, 1, sources * RANK, lanes), lambda e: (0, e, 0, 0)),
            whole_block((sources, tokens, width)),
        ],
        out_shape=[
            jax.ShapeDtypeStruct((cohort, experts, sources * RANK, lanes), bf16),
            jax.ShapeDtypeStruct((sources, tokens, width), bf16),
        ],
        scratch_shapes=[pltpu.VMEM((sources, experts * CAP, width), bf16)],
        compiler_params=call_params(),
        cost_estimate=pl.CostEstimate(
            flops=2 * experts * rows * width * inner_size * 2,
            bytes_accessed=experts * width * (inner_size * 2 + rows * 6),
            transcendentals=0,
        ),
        name="experts_post",
    )(
        slots, gates, down, down_first, down_second, picked, hidden, adj, inner, picked_grads,
        grad_inner_down, target,
    )


def shifted(array, axis, size, shift):
    return lax.ppermute(array, axis, [(i, (i + shift) % size) for i in range(size)])


def gather_shifted(array, axis, size):
    return [array] + [shifted(array, axis, size, r) for r in range(1, size)]


def return_shifted(blocks, axis, size):
    total = blocks[0].astype(f32)
    for r in range(1, size):
        total = total + shifted(blocks[r], axis, size, -r).astype(f32)
    return total


def flipped(array, axis, size, mask):
    return lax.ppermute(array, axis, [(i, i ^ mask) for i in range(size)])


def gather_cohort(array, size):
    place = jnp.arange(size, dtype=jnp.int32)
    if size != 8:
        return lax.all_gather(array, "ctx", axis=0, tiled=False), place
    half = array.shape[0] // 2
    near = flipped(array, "ctx", size, 2)
    far = flipped(array, "ctx", size, 4)
    low = flipped(near[:half], "ctx", size, 4)
    high = flipped(far[half:], "ctx", size, 2)
    mine = jnp.stack([array, near, far, jnp.concatenate([low, high], axis=0)])
    other = flipped(mine, "ctx", size, 1)
    blocks = jnp.concatenate([mine, other], axis=0)
    mask = place ^ lax.axis_index("ctx")
    return blocks, (mask & 1) * 4 + mask // 2


def head_columns(query, key, value):
    rows = query.shape[0]

    def split(array):
        return jnp.transpose(array.reshape(rows, PAIRED_ATTENDERS, -1), (1, 0, 2))

    parts = [split(key), split(value), split(query)]
    pad = HEAD_COLS - sum(p.shape[2] for p in parts)
    parts.append(jnp.zeros((PAIRED_ATTENDERS, rows, pad), query.dtype))
    return jnp.concatenate(parts, axis=2)


def body(
    tokens, out_grad, attn_gain, moe_gain, w_query, lock_projection, content_projection, w_out,
    sigmoid_matrices, widener_matrices, reducer_matrices, segment_ids, expert_routes,
    route_weights, adapter_index, query_first, query_second, key_first, lock_final_matrices,
    value_first, content_final_matrices, output_first, output_second, gate_first, gate_second,
    upward_first, upward_second, down_first, down_second,
):
    rows_in = tokens[0].astype(f32)
    count, width = rows_in.shape
    cohort = lax.axis_size("ctx")
    sources = lax.axis_size("exp")
    experts = sigmoid_matrices.shape[0]
    ctx = lax.axis_index("ctx")
    exp = lax.axis_index("exp")
    ways = cohort // PAIRED_ATTENDERS
    head = ctx // ways
    adapter = adapter_index[exp]

    def elected(table):
        return lax.dynamic_index_in_dim(table, adapter, 0, keepdims=False)

    full_out = lax.all_gather(w_out, ("ctx", "exp"), axis=0, tiled=True)
    head_w = head_columns(w_query, lock_projection, content_projection)
    to_all = jnp.broadcast_to(
        head_w[:, None], (PAIRED_ATTENDERS, ways * sources) + head_w.shape[1:]
    ).reshape((cohort * sources,) + head_w.shape[1:])
    own_w = lax.all_to_all(to_all, ("ctx", "exp"), 0, 0, tiled=True).reshape(width, HEAD_COLS)

    normed_in = normed(rows_in, attn_gain)[0].astype(bf16)
    factor_in = normed(rows_in, attn_gain)[1]
    x_blocks, place = gather_cohort(normed_in, cohort)
    segments = lax.all_gather(segment_ids[0].astype(bf16), "ctx", axis=0, tiled=True).astype(f32)
    seg_row, seg_col = segments[None, :], segments[:, None]
    order = jnp.concatenate([place, (ctx % ways)[None].astype(jnp.int32)])

    routes = expert_routes[0].astype(bf16)
    weight_high = route_weights[0].astype(bf16)
    weight_low = (route_weights[0] - weight_high.astype(f32)).astype(bf16)
    parcel = jnp.concatenate(
        [
            out_grad[0], routes, weight_high, weight_low,
            jnp.zeros((count, LANES - 3 * TOPK), bf16),
        ],
        axis=1,
    )
    parcels = jnp.concatenate(gather_shifted(parcel, "exp", sources), axis=0)
    full_in = lax.all_gather(
        jnp.concatenate([w_query, lock_projection, content_projection], axis=1),
        ("ctx", "exp"), axis=0, tiled=True,
    )
    attended_cols = ASKING_ATTENDERS * ATTENTION_EXTENT
    key_cols = PAIRED_ATTENDERS * ATTENTION_EXTENT

    extra = parcels[:, width:].astype(f32)
    all_routes = extra[:, :TOPK].astype(jnp.int32) - exp * experts
    all_gates = extra[:, TOPK : 2 * TOPK] + extra[:, 2 * TOPK : 3 * TOPK]
    hits = all_routes[None] == jnp.arange(experts, dtype=jnp.int32)[:, None, None]
    named = jnp.any(hits, axis=2)
    gates = jnp.sum(jnp.where(hits, all_gates[None], 0.0), axis=2)
    earlier = jnp.tril(jnp.ones((count, count), bf16), -1)
    rank = lax.dot_general(
        named.astype(bf16).reshape(experts * sources, count), earlier,
        (((1,), (1,)), ((), ())), preferred_element_type=f32,
    ).astype(jnp.int32).reshape(experts, sources, count)
    side = (jnp.arange(sources, dtype=jnp.int32) % 2 * CAP)[None, :, None]
    slots = jnp.where(named, (rank + side).reshape(experts, -1), -1)[:, None]
    gates = gates[:, None]
    rank = rank.reshape(experts, sources * count)
    places = jnp.arange(experts, dtype=jnp.int32)[:, None] * CAP + rank + 1
    target = jnp.sum(jnp.where(hits, places[:, :, None], 0), axis=0) - 1

    source_adapters = adapter_index[
        (exp - jnp.arange(sources, dtype=jnp.int32) + sources) % sources
    ]

    def chosen(table):
        taken = jnp.stack([
            lax.dynamic_index_in_dim(table, source_adapters[s], 0, keepdims=False)
            for s in range(sources)
        ], axis=1)
        return taken.reshape(experts, sources * RANK, table.shape[3])

    firsts = jnp.concatenate([chosen(gate_first), chosen(upward_first)], axis=1)
    gate_seconds, up_seconds = chosen(gate_second), chosen(upward_second)
    blank = jnp.zeros_like(gate_seconds)
    seconds = jnp.concatenate(
        [
            jnp.concatenate([gate_seconds, blank], axis=2),
            jnp.concatenate([blank, up_seconds], axis=2),
        ],
        axis=1,
    )
    down_firsts, down_seconds = chosen(down_first), chosen(down_second)

    picked_grads, grad_hidden, grad_inner_down = experts_pre(
        slots, gates, parcels, reducer_matrices, down_firsts, down_seconds
    )

    own_firsts = jnp.concatenate(
        [elected(query_first), elected(key_first), elected(value_first)], axis=0
    )
    own_firsts = jnp.pad(own_firsts, ((0, LANES - 3 * RANK), (0, 0)))

    def head_part(table):
        part = elected(table)
        size = part.shape[1] // PAIRED_ATTENDERS
        return lax.dynamic_slice_in_dim(part, head * size, size, 1)

    def placed(part, row, col):
        return jnp.pad(
            part, ((row, LANES - row - RANK), (col, HEAD_COLS - col - part.shape[1]))
        )

    own_seconds = (
        placed(head_part(query_second), 0, LANES)
        + placed(head_part(lock_final_matrices), RANK, 0)
        + placed(head_part(content_final_matrices), 2 * RANK, ATTENTION_EXTENT)
    )
    qkv, inner, attended_heads, lse = project_attend(
        order, x_blocks, own_w, own_firsts, own_seconds, seg_col, seg_row, ways
    )

    def to_tokens(array):
        got = lax.all_to_all(
            array.reshape(cohort, count, array.shape[1]), "ctx", 0, 0, tiled=True
        )
        if ways > 1:
            got = got.reshape(PAIRED_ATTENDERS, ways, count, -1).astype(f32).sum(1).astype(bf16)
        return got

    attended = jnp.transpose(to_tokens(attended_heads), (1, 0, 2)).reshape(count, attended_cols)
    out_first, out_second = elected(output_first), elected(output_second)
    inner_out = nt(attended, out_first).astype(bf16)
    mid = rows_in + nn(attended, full_out) + LOW_FACTORED * nn(inner_out, out_second)
    normed_mid_f, factor_mid = normed(mid, moe_gain)
    normed_mid = normed_mid_f.astype(bf16)

    x_all = jnp.concatenate(gather_shifted(normed_mid, "exp", sources), axis=0)
    picked, hidden, adj, inner_rows, grad_parts = experts_main(
        slots, x_all, firsts, seconds, sigmoid_matrices, widener_matrices, grad_hidden, target
    )
    grad_normed_mid = return_shifted(
        [grad_parts[r] for r in range(sources)], "exp", sources
    )
    tables, answer_parts = experts_post(
        slots, gates, reducer_matrices, down_firsts, down_seconds, picked, hidden, adj,
        inner_rows, picked_grads, grad_inner_down, target, cohort,
    )
    answers = return_shifted([answer_parts[r] for r in range(sources)], "exp", sources)
    block_out = (mid + answers).astype(bf16)[None]
    table_rows = lax.psum_scatter(tables, "ctx", scatter_dimension=0, tiled=False)

    grad_out = out_grad[0].astype(f32)
    grad_mid = grad_out + norm_back(mid, factor_mid, moe_gain, grad_normed_mid)
    grad_branch = grad_mid.astype(bf16)
    grad_inner_out = (LOW_FACTORED * nt(grad_branch, out_second)).astype(bf16)
    grad_attended = (nt(grad_branch, full_out) + nn(grad_inner_out, out_first)).astype(bf16)
    adj_heads = jnp.transpose(
        grad_attended.reshape(count, PAIRED_ATTENDERS, QUERY_COLS), (1, 0, 2)
    )
    if ways > 1:
        adj_heads = jnp.repeat(adj_heads, ways, axis=0)
    adj_all = lax.all_to_all(adj_heads, "ctx", 0, 0, tiled=True).reshape(-1, QUERY_COLS)
    grad_output_first = tn(grad_inner_out, attended)
    grad_output_second = LOW_FACTORED * tn(inner_out, grad_branch)

    grad_heads, grad_inner, grad_own_seconds = attend_back(
        order, qkv, adj_all, lse, own_seconds, inner, seg_col, seg_row, cohort, ways
    )
    grad_tokens = to_tokens(grad_heads)
    grad_own_firsts = first_grad(order, x_blocks, grad_inner)

    def flat(array):
        return jnp.transpose(array, (1, 0, 2)).reshape(count, -1)

    half = ATTENTION_EXTENT
    grad_key = flat(grad_tokens[:, :, :half])
    grad_value = flat(grad_tokens[:, :, half:LANES])
    grad_query = flat(grad_tokens[:, :, LANES : LANES + QUERY_COLS])
    grad_normed_in = nt(jnp.concatenate([grad_query, grad_key, grad_value], axis=1), full_in)
    for grad, first, second in (
        (grad_query, query_first, query_second),
        (grad_key, key_first, lock_final_matrices),
        (grad_value, value_first, content_final_matrices),
    ):
        grad_inner_in = (LOW_FACTORED * nt(grad, elected(second))).astype(bf16)
        grad_normed_in = grad_normed_in + nn(grad_inner_in, elected(first))
    tokens_grad = (
        grad_mid + norm_back(rows_in, factor_in, attn_gain, grad_normed_in)
    ).astype(bf16)[None]

    wide = width // cohort
    own = jnp.concatenate(
        [grad_own_firsts[: 3 * RANK], grad_output_first, grad_output_second], axis=0
    ).astype(bf16)
    pieces = jnp.transpose(own.reshape(5 * RANK, cohort, wide), (1, 0, 2))
    summed = lax.all_to_all(pieces, "ctx", 0, 0, tiled=True).astype(f32).sum(0).astype(bf16)
    span = max(wide, QUERY_COLS)
    seconds_in = grad_own_seconds.astype(bf16)
    query_part = seconds_in[:RANK, LANES : LANES + QUERY_COLS]
    key_part = seconds_in[RANK : 2 * RANK, :half]
    value_part = seconds_in[2 * RANK : 3 * RANK, half:LANES]

    def fit(array):
        return jnp.pad(array, ((0, 0), (0, span - array.shape[1])))

    slip = jnp.concatenate(
        [fit(summed), fit(query_part), fit(key_part), fit(value_part)],
        axis=0,
    )
    groups = jnp.stack(gather_shifted(slip, "exp", sources))
    gathered, spot = gather_cohort(groups.reshape(-1, span), cohort)
    gathered = gathered[spot].reshape(cohort, sources, 8 * RANK, span)
    choice = (
        source_adapters[:, None] == jnp.arange(NUM_CHOICES_X, dtype=jnp.int32)[None, :]
    ).astype(f32)

    def to_adapters(array):
        total = 0.0
        for source in range(sources):
            factor = choice[source].reshape((NUM_CHOICES_X,) + (1,) * (array.ndim - 1))
            total = total + factor * array[source][None].astype(f32)
        return total

    def wide_table(index):
        part = gathered[:, :, index * RANK : (index + 1) * RANK, :wide]
        return to_adapters(jnp.transpose(part, (1, 2, 0, 3)).reshape(sources, RANK, width))

    def slim_table(row, start, size):
        part = gathered[:, :, row : row + RANK, start : start + size].astype(f32)
        part = part.reshape(PAIRED_ATTENDERS, ways, sources, RANK, size).sum(1)
        return to_adapters(jnp.transpose(part, (1, 2, 0, 3)).reshape(sources, RANK, -1))

    query_table = slim_table(5 * RANK, 0, QUERY_COLS)
    key_table = slim_table(6 * RANK, 0, half)
    value_table = slim_table(7 * RANK, 0, half)

    inner_size = sigmoid_matrices.shape[2]
    slim = inner_size // cohort
    table_rows = jnp.transpose(
        table_rows.reshape(experts, sources, RANK, -1), (1, 0, 2, 3)
    )

    def expert_table(start, size):
        return to_adapters(table_rows[..., start : start + size])

    return (
        block_out,
        tokens_grad,
        wide_table(0),
        query_table,
        wide_table(1),
        key_table,
        wide_table(2),
        value_table,
        wide_table(3),
        wide_table(4),
        expert_table(0, wide),
        expert_table(3 * wide, slim),
        expert_table(wide, wide),
        expert_table(3 * wide + slim, slim),
        expert_table(3 * wide + 2 * slim, slim),
        expert_table(2 * wide, wide),
    )


def solution(mesh):
    sharded = P("exp", "ctx", None)
    rows = P(("ctx", "exp"), None)
    table = P(None, "exp", None, None)
    expert = P("exp", None, None)
    in_specs = (
        (sharded, sharded, P(), P())
        + (rows,) * 4
        + (expert,) * 3
        + (P("exp", "ctx"), sharded, sharded, P())
        + (P(),) * 8
        + (table,) * 6
    )
    out_specs = (sharded, sharded) + (P(),) * 8 + (P(None, "exp", None, "ctx"),) * 6
    return jax.shard_map(body, mesh=mesh, in_specs=in_specs, out_specs=out_specs, check_vma=False)
```

time: 1780 us -> 547 us (0.31)
  local copies, waits for them, and re-layouts: 745 us -> 111 us
  waiting for transfers between devices: 693 us -> 128 us
  matrix products: 212 us -> 22 us
  Pallas kernels: 0 us -> 116 us
  starting transfers between devices: 23.2 us -> 58 us
  other arithmetic: 53.6 us -> 73 us
    unnamed x202 -> x153, local copies, waits for them, and re-layouts: 650 us -> 7.15 us
    all_gather x6 -> x2, waiting for transfers between devices: 283 us -> 0.02 us  [the longest x1 0.02 us: body(): full_out = lax.all_gather(w_out, ('ctx', 'exp'), axis=0, tiled=True)]
    all_to_all x4 -> x5, waiting for transfers between devices: 288 us -> 19.9 us  [the longest x1 7.71 us: body(): lax.all_to_all(adj_heads, 'ctx', 0, 0, tiled=True).reshape(-1, QUERY_COLS)]
    dot_general x69 -> x13, matrix products: 212 us -> 22 us  [the longest x4 11.9 us: nt(): lax.dot_general(left, right, (((1,), (1,)), ((), ())), preferred_element_...]
    psum x1 -> x0, waiting for transfers between devices: 119 us -> none  [body(): lax.psum((placed[0], placed[1], placed[2], placed[3], placed[4], placed[5...]
    pallas_call x0 -> x6, Pallas kernels: none -> 116 us  [the longest x1 36.3 us: experts_main(): pl.pallas_call(functools.partial(experts_main_kernel, sources), grid=(exp...]
    ppermute x0 -> x25, waiting for transfers between devices: none -> 107 us  [the longest x15 90.2 us: shifted(): lax.ppermute(array, axis, [(i, (i + shift) % size) for i in range(size)])]
    gather x8 -> x2, local copies, waits for them, and re-layouts: 41.4 us -> 2.59 us  [the longest x1 1.95 us: body(): gathered = gathered[spot].reshape(cohort, sources, 8 * RANK, span)]
  transfers between devices with their start and end apart: 19 -> 33, of which waited for: 9 -> 17; matrix products, arithmetic and copies ran while one was open for 50% -> 36% of each run, Pallas kernels for 0% -> 21%
where the time goes in v1:
time: 547 us; the launch traced here: 541 us
  waiting for transfers between devices  128 us (23%)
  Pallas kernels  116 us (21%)
  local copies, waits for them, and re-layouts  111 us (20%)
  other arithmetic  73 us (13%)
  starting transfers between devices  58 us (11%)
  between operations  25 us (5%)
  matrix products  22 us (4%)
  blocking collectives  9 us (2%)
    ppermute x15, waiting for transfers between devices, shifted(): lax.ppermute(array, axis, [(i, (i + shift) % size) for i in range(size)])  90.2 us
    convert_element_type x20, local copies, waits for them, and re-layouts, to_adapters(): total = total + factor * array[source][None].astype(f32)  38.6 us
    pallas_call x1, Pallas kernels, experts_main(): pl.pallas_call(functools.partial(experts_main_kernel, sources), grid=(exp...  36.3 us
    ppermute x15, starting transfers between devices, shifted(): lax.ppermute(array, axis, [(i, (i + shift) % size) for i in range(size)])  26.1 us
    pallas_call x1, Pallas kernels, experts_post(): pl.pallas_call(functools.partial(experts_post_kernel, sources, cohort), g...  23.8 us
    mul x13, local copies, waits for them, and re-layouts, to_adapters(): total = total + factor * array[source][None].astype(f32)  22 us
    pallas_call x1, Pallas kernels, experts_pre(): pl.pallas_call(functools.partial(experts_pre_kernel, sources), grid=(expe...  19.5 us
    pallas_call x1, Pallas kernels, project_attend(): pl.pallas_call(functools.partial(project_attend_kernel, blocks, ways), gr...  18 us
  transfers between devices with their start and end apart: 33, of which 17 were waited for; matrix products, arithmetic and copies ran while one was open for 36% of the time, Pallas kernels for 21%

profile of v1, /device:TPU:0, one launch (start us, length us, event | category | flops | bytes accessed | tf_op | source)
XLA Modules:
  0.0 540.9 jit_solution(4243470196618484184)
XLA Ops:
  24.4 3.5 all-to-all-start
  38.1 9.0 %all-gather = bf16[1,1024]{1,0:T(2,128)(2,1)S(1)} all-gather(bf16[1,128]{1,0:T(2,128)(2,1)S(1)} %convert_element_type.385), channel_id=2, replica_groups=mesh['ctx'=8,'exp'=4] {'ctx'}, dimensions={1}, use_global_device_ids=true | all-gather | bytes 2304 | tf_op jit(solution)/shard_map/all_gather | solution.py:626
  68.9 3.9 pad_maximum_fusion.firsts
  78.1 4.3 collective-permute-done.2
  92.7 4.7 all-to-all-done
  97.4 18.0 %project_attend.1 = (bf16[1024,384]{1,0:T(8,128)(2,1)}, bf16[1024,128]{1,0:T(8,128)(2,1)}, bf16[1024,192]{1,0:T(8,128)(2,1)}, f32[8,1024]{1,0:T(8,128)}) custom-call(s32[9]{0:T(128)} %pad_add_fusion.1.order_ref, bf16[8,128,1536]{2,1,0:T(8,128)(2,1)} %constant_dynamic-update-slice_fusion.x_ref, bf16[1536,384]{1,0:T(8,128)(2,1)} %bitcast.8.w_ref, ...), custom_call_target="tpu_custom_call" | custom-call | flops 3758096384 | bytes 6291456 | tf_op jit(solution)/shard_map/project_attend/pallas_call | solution.py:129
  117.4 6.0 %all-to-all-start.1 = ((bf16[8,128,192]{1,2,0:T(8,128)(2,1)}), bf16[8,128,192]{1,2,0:T(8,128)(2,1)S(1)}, u32[]{:S(2)}, u32[]{:S(2)}) async-start(bf16[8,128,192]{1,2,0:T(8,128)(2,1)} %copy.250), calls=%async_computation.1 | async-start | bytes 786432 | tf_op jit(solution)/shard_map/all_to_all | solution.py:718
  123.6 19.5 %experts_pre.1 = (bf16[10,192,1536]{2,1,0:T(8,128)(2,1)}, f32[10,192,512]{2,1,0:T(8,128)}, bf16[10,192,64]{2,1,0:T(8,128)(2,1)}) custom-call(s32[10,1,512]{2,1,0:T(1,128)} %copy_select_fusion.slot_ref, f32[10,1,512]{2,1,0:T(1,128)} %broadcast_in_dim.94.gate_ref, bf16[512,1664]{1,0:T(8,128)(2,1)} %copy-done.11, bf16[10,512,1536]{2,1,0:T(8,128)(2,1)} %down_ref.3, ...), custom_call_target="tpu_custom_call" | custom-call | flops 6039797760 | bytes 21626880 | tf_op jit(solution)/shard_map/experts_pre/pallas_call | solution.py:432
  148.7 3.7 collective-permute-start.10
  154.9 30.6 %collective-permute-done.10 = bf16[128,1536]{1,0:T(8,128)(2,1)S(1)} collective-permute-done((bf16[128,1536]{1,0:T(8,128)(2,1)S(1)}, bf16[128,1536]{1,0:T(8,128)(2,1)S(1)}, u32[]{:S(2)}, u32[]{:S(2)}) %collective-permute-start.10) | collective-permute-done | bytes 393248 | tf_op jit(solution)/shard_map/ppermute | solution.py:549
  186.9 22.7 %collective-permute-done.9 = bf16[128,1536]{1,0:T(8,128)(2,1)} collective-permute-done((bf16[128,1536]{1,0:T(8,128)(2,1)S(1)}, bf16[128,1536]{1,0:T(8,128)(2,1)}, u32[]{:S(2)}, u32[]{:S(2)}) %collective-permute-start.9) | collective-permute-done | bytes 393248 | tf_op jit(solution)/shard_map/ppermute | solution.py:549
  211.8 36.3 %experts_main.1 = (bf16[10,192,1536]{2,1,0:T(8,128)(2,1)}, bf16[10,192,512]{2,1,0:T(8,128)(2,1)}, bf16[10,192,1024]{2,1,0:T(8,128)(2,1)}, bf16[10,192,256]{2,1,0:T(8,128)(2,1)}, bf16[4,128,1536]{2,1,0:T(8,128)(2,1)}) custom-call(s32[10,1,512]{2,1,0:T(1,128)} %copy_select_fusion.slot_ref, bf16[512,1536]{1,0:T(8,128)(2,1)} %pad_maximum_fusion.6.x_ref, ...), custom_call_target="tpu_custom_call" | custom-call | flops 15099494400 | bytes 43253760 | tf_op jit(solution)/shard_map/experts_main/pallas_call | solution.py:468
  252.6 23.8 %experts_post.1 = (bf16[8,10,64,768]{3,2,1,0:T(8,128)(2,1)}, bf16[4,128,1536]{2,1,0:T(8,128)(2,1)}) custom-call(s32[10,1,512]{2,1,0:T(1,128)} %copy_select_fusion.slot_ref, f32[10,1,512]{2,1,0:T(1,128)} %broadcast_in_dim.94.gate_ref, bf16[10,512,1536]{2,1,0:T(8,128)(2,1)} %down_ref.3, bf16[10,64,512]{2,1,0:T(8,128)(2,1)} %bitcast.465, ...), custom_call_target="tpu_custom_call" | custom-call | flops 6039797760 | bytes 33423360 | tf_op jit(solution)/shard_map/experts_post/pallas_call | solution.py:515
  287.6 6.1 %collective-permute-done.11 = bf16[128,1536]{1,0:T(8,128)(2,1)} collective-permute-done((bf16[128,1536]{1,0:T(8,128)(2,1)}, bf16[128,1536]{1,0:T(8,128)(2,1)}, u32[]{:S(2)}, u32[]{:S(2)}) %collective-permute-start.11) | collective-permute-done | bytes 393248 | tf_op jit(solution)/shard_map/ppermute | solution.py:549
  293.6 25.3 %collective-permute-done.12 = bf16[128,1536]{1,0:T(8,128)(2,1)} collective-permute-done((bf16[128,1536]{1,0:T(8,128)(2,1)}, bf16[128,1536]{1,0:T(8,128)(2,1)}, u32[]{:S(2)}, u32[]{:S(2)}) %collective-permute-start.12) | collective-permute-done | bytes 393248 | tf_op jit(solution)/shard_map/ppermute | solution.py:549
  321.8 4.0 fusion.130
  328.9 3.8 all-to-all-start.2
  333.3 7.7 %all-to-all-done.2 = bf16[8,128,192]{1,2,0:T(8,128)(2,1)S(1)} async-done(((bf16[8,128,192]{1,2,0:T(8,128)(2,1)}), bf16[8,128,192]{1,2,0:T(8,128)(2,1)S(1)}, u32[]{:S(2)}, u32[]{:S(2)}) %all-to-all-start.2) | async-done | bytes 393248 | tf_op jit(solution)/shard_map/all_to_all | solution.py:757
  342.1 11.0 %attend_back.1 = (bf16[1024,384]{1,0:T(8,128)(2,1)}, bf16[1024,128]{1,0:T(8,128)(2,1)}, f32[128,384]{1,0:T(8,128)}) custom-call(s32[9]{0:T(128)} %pad_add_fusion.1.order_ref, bf16[1024,384]{1,0:T(8,128)(2,1)} %get-tuple-element.43.qkv_ref, bf16[1024,192]{1,0:T(8,128)(2,1)} %bitcast.489, f32[8,1024]{1,0:T(8,128)} %get-tuple-element.44.lse_ref, ...), custom_call_target="tpu_custom_call" | custom-call | flops 5368709120 | bytes 2048000 | tf_op jit(solution)/shard_map/attend_back/pallas_call | solution.py:219
  353.1 7.2 %first_grad.1 = f32[128,1536]{1,0:T(8,128)} custom-call(s32[9]{0:T(128)} %pad_add_fusion.1.order_ref, bf16[8,128,1536]{2,1,0:T(8,128)(2,1)} %constant_dynamic-update-slice_fusion.x_ref, bf16[1024,128]{1,0:T(8,128)(2,1)} %get-tuple-element.47.grad_inner_ref), custom_call_target="tpu_custom_call" | custom-call | flops 402653184 | bytes 3145728 | tf_op jit(solution)/shard_map/first_grad/pallas_call | solution.py:263
  365.9 7.5 %all-to-all-done.4 = bf16[8,80,192]{2,1,0:T(8,128)(2,1)S(1)} async-done(((bf16[8,80,192]{2,1,0:T(8,128)(2,1)}), bf16[8,80,192]{2,1,0:T(8,128)(2,1)S(1)}, u32[]{:S(2)}, u32[]{:S(2)}) %all-to-all-start.4) | async-done | bytes 245792 | tf_op jit(solution)/shard_map/all_to_all | solution.py:791
  385.5 4.4 all-to-all-start.3
  394.2 9.3 %collective-permute-done.22 = bf16[256,192]{0,1:T(8,128)(2,1)S(1)} collective-permute-done((bf16[256,192]{0,1:T(8,128)(2,1)S(1)}, bf16[256,192]{0,1:T(8,128)(2,1)S(1)}, u32[]{:S(2)}, u32[]{:S(2)}) %collective-permute-start.22) | collective-permute-done | bytes 98336 | tf_op jit(solution)/shard_map/ppermute | solution.py:564
  424.0 4.5 fusion.139
  435.2 6.4 %slice_bitcast_fusion = (bf16[4,16,8,192]{1,0,3,2:T(4,128)(2,1)}, bf16[4,16,8,192]{1,0,3,2:T(4,128)(2,1)}, bf16[4,16,8,192]{1,0,3,2:T(4,128)(2,1)}, bf16[4,16,8,...) fusion(bf16[8,4,128,192]{2,1,3,0:T(4,128)(2,1)S(1)} %reshape.662), kind=kLoop, calls=%fused_computation.24 | loop fusion | flops 98304 | bytes 2555904 | tf_op jit(solution)/shard_map/transpose | solution.py:821
  441.6 3.7 fusion.138
  453.4 3.5 slice_convert_fusion.15
  465.1 3.7 slice_convert_fusion.3
  477.1 3.5 slice_convert_fusion.19
  488.8 3.5 slice_convert_fusion.11
  500.5 3.5 slice_convert_fusion.7
  517.0 5.9 %fusion.36 = f32[128,1536]{1,0:T(8,128)S(1)} fusion(bf16[1536,2560]{1,0:T(8,128)(2,1)} %all-gather.6.cloned.1.call-done, bf16[128,512]{0,1:T(8,128)(2,1)S(1)} %bitcast.475, bf16[128,512]{0,1:T(8,128)(2,1)S(1)} %bitcast.478, bf16[128,1536]{0,1:T(8,128)(2,1)S(1)} %bitcast.436), kind=kOutput, calls=%fused_computation.111 | convolution fusion | flops 1008599040 | bytes 9306112 | tf_op jit(solution)/shard_map/dot_general | solution.py:39
  (373 shorter events, 205.2 us)
Async XLA Ops:
  7.2 136.9 %all-gather.4.cloned.1.call-start = ((), (), s32[]{:S(2)}) async-start(), calls=%async_computation.6 | async-start | bytes 4866048 | tf_op jit(solution)/shard_map/all_gather | solution.py:616
  11.5 65.1 %collective-permute-start.5 = (bf16[128,1664]{1,0:T(8,128)(2,1)}, bf16[128,1664]{1,0:T(8,128)(2,1)}, u32[]{:S(2)}, u32[]{:S(2)}) collective-permute-start(bf16[128,1664]{1,0:T(8,128)(2,1)} %concatenate.67), channel_id=1, source_target_pairs={{0,1},{1,2},{2,3},{3,0},{4,5},{5,6},{6,7},{7,4},{8,9},{9,10},{10,1... | collective-permute-start | bytes 1277960 | tf_op jit(solution)/shard_map/ppermute | solution.py:549
  14.5 62.1 %collective-permute-start.6 = (bf16[128,1664]{1,0:T(8,128)(2,1)}, bf16[128,1664]{1,0:T(8,128)(2,1)}, u32[]{:S(2)}, u32[]{:S(2)}) collective-permute-start(bf16[128,1664]{1,0:T(8,128)(2,1)} %concatenate.67), channel_id=1, source_target_pairs={{0,2},{1,3},{2,0},{3,1},{4,6},{5,7},{6,4},{7,5},{8,10},{9,11},{10,... | collective-permute-start | bytes 1277960 | tf_op jit(solution)/shard_map/ppermute | solution.py:549
  17.1 59.5 %collective-permute-start.7 = (bf16[128,1664]{1,0:T(8,128)(2,1)}, bf16[128,1664]{1,0:T(8,128)(2,1)}, u32[]{:S(2)}, u32[]{:S(2)}) collective-permute-start(bf16[128,1664]{1,0:T(8,128)(2,1)} %concatenate.67), channel_id=1, source_target_pairs={{0,3},{1,0},{2,1},{3,2},{4,7},{5,4},{6,5},{7,6},{8,11},{9,8},{10,9... | collective-permute-start | bytes 1277960 | tf_op jit(solution)/shard_map/ppermute | solution.py:549
  19.5 53.3 %collective-permute-start = (bf16[128,1536]{1,0:T(8,128)(2,1)}, bf16[128,1536]{1,0:T(8,128)(2,1)S(1)}, u32[]{:S(2)}, u32[]{:S(2)}) collective-permute-start(bf16[128,1536]{1,0:T(8,128)(2,1)} %fusion.16), channel_id=1, source_target_pairs={{0,8},{4,12},{8,0},{12,4},{16,24},{20,28},{24,16},{28,20},{1,9},{5... | collective-permute-start | bytes 1179656 | tf_op jit(solution)/shard_map/ppermute | solution.py:564
  21.0 53.4 %collective-permute-start.1 = (bf16[128,1536]{1,0:T(8,128)(2,1)}, bf16[128,1536]{1,0:T(8,128)(2,1)S(1)}, u32[]{:S(2)}, u32[]{:S(2)}) collective-permute-start(bf16[128,1536]{1,0:T(8,128)(2,1)} %fusion.16), channel_id=1, source_target_pairs={{0,16},{4,20},{8,24},{12,28},{16,0},{20,4},{24,8},{28,12},{1,17},{... | collective-permute-start | bytes 1179656 | tf_op jit(solution)/shard_map/ppermute | solution.py:564
  24.4 73.0 %all-to-all-start = ((bf16[32,48,384]{2,1,0:T(8,128)(2,1)}), bf16[32,48,384]{2,1,0:T(8,128)(2,1)}, u32[]{:S(2)}, u32[]{:S(2)}) async-start(bf16[32,48,384]{2,1,0:T(8,128)(2,1)} %bitcast.7), calls=%async_computation | async-start | bytes 2359296 | tf_op jit(solution)/shard_map/all_to_all | solution.py:621
  27.9 489.1 %all-gather.6.cloned.1.call-start = ((), (), s32[]{:S(2)}) async-start(), calls=%async_computation.7 | async-start | bytes 8110080 | tf_op jit(solution)/shard_map/all_gather | solution.py:641
  72.9 9.6 %collective-permute-start.2 = (bf16[64,1536]{1,0:T(8,128)(2,1)S(1)}, bf16[64,1536]{1,0:T(8,128)(2,1)S(1)}, u32[]{:S(2)}, u32[]{:S(2)}) collective-permute-start(bf16[64,1536]{1,0:T(8,128)(2,1)S(1)} %slice.519), channel_id=1, source_target_pairs={{0,16},{4,20},{8,24},{12,28},{16,0},{20,4},{24,8},{28,12},{1,17},{... | collective-permute-start | bytes 589832 | tf_op jit(solution)/shard_map/ppermute | solution.py:564
  74.4 10.5 %collective-permute-start.3 = (bf16[64,1536]{1,0:T(8,128)(2,1)S(1)}, bf16[64,1536]{1,0:T(8,128)(2,1)S(1)}, u32[]{:S(2)}, u32[]{:S(2)}) collective-permute-start(bf16[64,1536]{1,0:T(8,128)(2,1)S(1)} %slice.520), channel_id=1, source_target_pairs={{0,8},{4,12},{8,0},{12,4},{16,24},{20,28},{24,16},{28,20},{1,9},{5... | collective-permute-start | bytes 589832 | tf_op jit(solution)/shard_map/ppermute | solution.py:564
  86.3 3.8 collective-permute-start.4
  117.4 25.8 %all-to-all-start.1 = ((bf16[8,128,192]{1,2,0:T(8,128)(2,1)}), bf16[8,128,192]{1,2,0:T(8,128)(2,1)S(1)}, u32[]{:S(2)}, u32[]{:S(2)}) async-start(bf16[8,128,192]{1,2,0:T(8,128)(2,1)} %copy.250), calls=%async_computation.1 | async-start | bytes 786432 | tf_op jit(solution)/shard_map/all_to_all | solution.py:718
  123.4 404.7 %reduce-scatter.2.cloned.1.call-start = ((), (), s32[]{:S(2)}) async-start(), calls=%async_computation.8 | async-start | bytes 8847360 | tf_op jit(solution)/shard_map/reduce_scatter | solution.py:745
  148.7 36.8 %collective-permute-start.10 = (bf16[128,1536]{1,0:T(8,128)(2,1)S(1)}, bf16[128,1536]{1,0:T(8,128)(2,1)S(1)}, u32[]{:S(2)}, u32[]{:S(2)}) collective-permute-start(bf16[128,1536]{1,0:T(8,128)(2,1)S(1)} %multiply_convert_fusion), channel_id=1, source_target_pairs={{0,3},{1,0},{2,1},{3,2},{4,7},{5,4},{6,5},{7,6},{8,11},{9,8},{10,9... | collective-permute-start | bytes 1179656 | tf_op jit(solution)/shard_map/ppermute | solution.py:549
  152.3 34.5 %collective-permute-start.8 = (bf16[128,1536]{1,0:T(8,128)(2,1)S(1)}, bf16[128,1536]{1,0:T(8,128)(2,1)S(1)}, u32[]{:S(2)}, u32[]{:S(2)}) collective-permute-start(bf16[128,1536]{1,0:T(8,128)(2,1)S(1)} %multiply_convert_fusion), channel_id=1, source_target_pairs={{0,1},{1,2},{2,3},{3,0},{4,5},{5,6},{6,7},{7,4},{8,9},{9,10},{10,1... | collective-permute-start | bytes 1179656 | tf_op jit(solution)/shard_map/ppermute | solution.py:549
  152.5 57.0 %collective-permute-start.9 = (bf16[128,1536]{1,0:T(8,128)(2,1)S(1)}, bf16[128,1536]{1,0:T(8,128)(2,1)}, u32[]{:S(2)}, u32[]{:S(2)}) collective-permute-start(bf16[128,1536]{1,0:T(8,128)(2,1)S(1)} %multiply_convert_fusion), channel_id=1, source_target_pairs={{0,2},{1,3},{2,0},{3,1},{4,6},{5,7},{6,4},{7,5},{8,10},{9,11},{10,... | collective-permute-start | bytes 1179656 | tf_op jit(solution)/shard_map/ppermute | solution.py:549
  250.3 32.8 %collective-permute-start.14 = (bf16[128,1536]{1,0:T(8,128)(2,1)}, bf16[128,1536]{1,0:T(8,128)(2,1)S(1)}, u32[]{:S(2)}, u32[]{:S(2)}) collective-permute-start(bf16[128,1536]{1,0:T(8,128)(2,1)} %get-tuple-element.98), channel_id=1, source_target_pairs={{0,3},{1,0},{2,1},{3,2},{4,7},{5,4},{6,5},{7,6},{8,11},{9,8},{10,9... | collective-permute-start | bytes 1179656 | tf_op jit(solution)/shard_map/ppermute | solution.py:549
  252.1 34.0 %collective-permute-start.15 = (bf16[128,1536]{1,0:T(8,128)(2,1)}, bf16[128,1536]{1,0:T(8,128)(2,1)S(1)}, u32[]{:S(2)}, u32[]{:S(2)}) collective-permute-start(bf16[128,1536]{1,0:T(8,128)(2,1)} %get-tuple-element.100), channel_id=1, source_target_pairs={{0,2},{1,3},{2,0},{3,1},{4,6},{5,7},{6,4},{7,5},{8,10},{9,11},{10,... | collective-permute-start | bytes 1179656 | tf_op jit(solution)/shard_map/ppermute | solution.py:549
  252.1 34.0 %collective-permute-start.16 = (bf16[128,1536]{1,0:T(8,128)(2,1)S(1)}, bf16[128,1536]{1,0:T(8,128)(2,1)S(1)}, u32[]{:S(2)}, u32[]{:S(2)}) collective-permute-start(bf16[128,1536]{1,0:T(8,128)(2,1)S(1)} %get-tuple-element.99), channel_id=1, source_target_pairs={{0,1},{1,2},{2,3},{3,0},{4,5},{5,6},{6,7},{7,4},{8,9},{9,10},{10,1... | collective-permute-start | bytes 1179656 | tf_op jit(solution)/shard_map/ppermute | solution.py:549
  278.7 15.0 %collective-permute-start.11 = (bf16[128,1536]{1,0:T(8,128)(2,1)}, bf16[128,1536]{1,0:T(8,128)(2,1)}, u32[]{:S(2)}, u32[]{:S(2)}) collective-permute-start(bf16[128,1536]{1,0:T(8,128)(2,1)} %get-tuple-element.101), channel_id=1, source_target_pairs={{0,3},{1,0},{2,1},{3,2},{4,7},{5,4},{6,5},{7,6},{8,11},{9,8},{10,9... | collective-permute-start | bytes 1179656 | tf_op jit(solution)/shard_map/ppermute | solution.py:549
  281.9 37.0 %collective-permute-start.12 = (bf16[128,1536]{1,0:T(8,128)(2,1)}, bf16[128,1536]{1,0:T(8,128)(2,1)}, u32[]{:S(2)}, u32[]{:S(2)}) collective-permute-start(bf16[128,1536]{1,0:T(8,128)(2,1)} %get-tuple-element.103), channel_id=1, source_target_pairs={{0,2},{1,3},{2,0},{3,1},{4,6},{5,7},{6,4},{7,5},{8,10},{9,11},{10,... | collective-permute-start | bytes 1179656 | tf_op jit(solution)/shard_map/ppermute | solution.py:549
  283.1 35.9 %collective-permute-start.13 = (bf16[128,1536]{1,0:T(8,128)(2,1)}, bf16[128,1536]{1,0:T(8,128)(2,1)S(1)}, u32[]{:S(2)}, u32[]{:S(2)}) collective-permute-start(bf16[128,1536]{1,0:T(8,128)(2,1)} %get-tuple-element.102), channel_id=1, source_target_pairs={{0,1},{1,2},{2,3},{3,0},{4,5},{5,6},{6,7},{7,4},{8,9},{9,10},{10,1... | collective-permute-start | bytes 1179656 | tf_op jit(solution)/shard_map/ppermute | solution.py:549
  328.9 12.1 %all-to-all-start.2 = ((bf16[8,128,192]{1,2,0:T(8,128)(2,1)}), bf16[8,128,192]{1,2,0:T(8,128)(2,1)S(1)}, u32[]{:S(2)}, u32[]{:S(2)}) async-start(bf16[8,128,192]{1,2,0:T(8,128)(2,1)} %bitcast.74), calls=%async_computation.2 | async-start | bytes 786432 | tf_op jit(solution)/shard_map/all_to_all | solution.py:757
  362.3 11.0 %all-to-all-start.4 = ((bf16[8,80,192]{2,1,0:T(8,128)(2,1)}), bf16[8,80,192]{2,1,0:T(8,128)(2,1)S(1)}, u32[]{:S(2)}, u32[]{:S(2)}) async-start(bf16[8,80,192]{2,1,0:T(8,128)(2,1)} %maximum_bitcast_fusion.1), calls=%async_computation.4 | async-start | bytes 655360 | tf_op jit(solution)/shard_map/all_to_all | solution.py:791
  373.4 6.8 %collective-permute-start.17 = (bf16[128,192]{1,0:T(8,128)(2,1)S(1)}, bf16[128,192]{1,0:T(8,128)(2,1)S(1)}, u32[]{:S(2)}, u32[]{:S(2)}) collective-permute-start(bf16[128,192]{1,0:T(8,128)(2,1)S(1)} %fusion.65), channel_id=1, source_target_pairs={{0,1},{1,2},{2,3},{3,0},{4,5},{5,6},{6,7},{7,4},{8,9},{9,10},{10,1... | collective-permute-start | bytes 147464 | tf_op jit(solution)/shard_map/ppermute | solution.py:549
  375.0 6.0 %collective-permute-start.18 = (bf16[128,192]{1,0:T(8,128)(2,1)S(1)}, bf16[128,192]{1,0:T(8,128)(2,1)S(1)}, u32[]{:S(2)}, u32[]{:S(2)}) collective-permute-start(bf16[128,192]{1,0:T(8,128)(2,1)S(1)} %fusion.65), channel_id=1, source_target_pairs={{0,2},{1,3},{2,0},{3,1},{4,6},{5,7},{6,4},{7,5},{8,10},{9,11},{10,... | collective-permute-start | bytes 147464 | tf_op jit(solution)/shard_map/ppermute | solution.py:549
  377.0 4.8 collective-permute-start.19
  382.0 8.1 %collective-permute-start.20 = (bf16[512,192]{0,1:T(8,128)(2,1)S(1)}, bf16[512,192]{0,1:T(8,128)(2,1)S(1)}, u32[]{:S(2)}, u32[]{:S(2)}) collective-permute-start(bf16[512,192]{0,1:T(8,128)(2,1)S(1)} %copy.302), channel_id=1, source_target_pairs={{0,8},{4,12},{8,0},{12,4},{16,24},{20,28},{24,16},{28,20},{1,9},{5... | collective-permute-start | bytes 589832 | tf_op jit(solution)/shard_map/ppermute | solution.py:564
  382.9 9.2 %collective-permute-start.21 = (bf16[512,192]{0,1:T(8,128)(2,1)S(1)}, bf16[512,192]{0,1:T(8,128)(2,1)S(1)}, u32[]{:S(2)}, u32[]{:S(2)}) collective-permute-start(bf16[512,192]{0,1:T(8,128)(2,1)S(1)} %copy.302), channel_id=1, source_target_pairs={{0,16},{4,20},{8,24},{12,28},{16,0},{20,4},{24,8},{28,12},{1,17},{... | collective-permute-start | bytes 589832 | tf_op jit(solution)/shard_map/ppermute | solution.py:564
  385.5 20.1 %all-to-all-start.3 = ((bf16[8,128,384]{1,2,0:T(8,128)(2,1)}), bf16[8,128,384]{1,2,0:T(8,128)(2,1)}, u32[]{:S(2)}, u32[]{:S(2)}) async-start(bf16[8,128,384]{1,2,0:T(8,128)(2,1)} %copy.260), calls=%async_computation.3 | async-start | bytes 1572864 | tf_op jit(solution)/shard_map/all_to_all | solution.py:718
  390.1 13.5 %collective-permute-start.22 = (bf16[256,192]{0,1:T(8,128)(2,1)S(1)}, bf16[256,192]{0,1:T(8,128)(2,1)S(1)}, u32[]{:S(2)}, u32[]{:S(2)}) collective-permute-start(bf16[256,192]{0,1:T(8,128)(2,1)S(1)} %slice.532), channel_id=1, source_target_pairs={{0,16},{4,20},{8,24},{12,28},{16,0},{20,4},{24,8},{28,12},{1,17},{... | collective-permute-start | bytes 294920 | tf_op jit(solution)/shard_map/ppermute | solution.py:564
  392.7 10.9 %collective-permute-start.23 = (bf16[256,192]{0,1:T(8,128)(2,1)S(1)}, bf16[256,192]{0,1:T(8,128)(2,1)S(1)}, u32[]{:S(2)}, u32[]{:S(2)}) collective-permute-start(bf16[256,192]{0,1:T(8,128)(2,1)S(1)} %slice.533), channel_id=1, source_target_pairs={{0,8},{4,12},{8,0},{12,4},{16,24},{20,28},{24,16},{28,20},{1,9},{5... | collective-permute-start | bytes 294920 | tf_op jit(solution)/shard_map/ppermute | solution.py:564
  (74 other events, 540.2 us)
Sparse Core Ops, SparseCore 0:
  10.9 92.2 all-gather.3
  106.6 98.9 all-gather.5
  283.2 72.2 reduce-scatter.1
